TPU v7x, 128 devices: a whole 4x4x4 slice. The times are simulated.
128 devices in a mesh: tower: 2 (over core), dp: 64 (over z, x, y).
Axes of the slice: x: 4, y: 4, z: 4, core: 2. Of those that a mesh axis runs over, the one named last changes fastest.
Arguments:
- image_tokens: bfloat16 [1024, 50, 768], P(('tower', 'dp')), may hold values from -6 to 6
- image_first_gain: float32 [768], replicated, may hold values from 0.5 to 1.5
- image_first_shift: float32 [768], replicated, may hold values from -3 to 3
- image_joint_weight: bfloat16 [768, 2304], replicated, may hold values from -0.21875 to 0.21875
- image_output_weight: bfloat16 [768, 768], replicated, may hold values from -1.25 to 1.25
- image_second_gain: float32 [768], replicated, may hold values from 0.5 to 1.5
- image_second_shift: float32 [768], replicated, may hold values from -3 to 3
- image_widen_weight: bfloat16 [768, 3072], replicated, may hold values from -0.21875 to 0.21875
- image_narrow_weight: bfloat16 [3072, 768], replicated, may hold values from -0.109375 to 0.109375
- image_final_gain: float32 [768], replicated, may hold values from 0.5 to 1.5
- image_final_shift: float32 [768], replicated, may hold values from -3 to 3
- image_projection: bfloat16 [768, 512], replicated, may hold values from -0.21875 to 0.21875
- image_block_out_grad: bfloat16 [1024, 50, 768], P(('tower', 'dp')), may hold values from -0.00018310547 to 0.00018310547
- text_tokens: bfloat16 [1024, 77, 512], P(('tower', 'dp')), may hold values from -6 to 6
- caption_lengths: int32 [1024], P(('tower', 'dp')), may hold values from 5 to 77, as said below
- text_first_gain: float32 [512], replicated, may hold values from 0.5 to 1.5
- text_first_shift: float32 [512], replicated, may hold values from -3 to 3
- text_joint_weight: bfloat16 [512, 1536], replicated, may hold values from -0.25 to 0.25
- text_output_weight: bfloat16 [512, 512], replicated, may hold values from -1 to 1
- text_second_gain: float32 [512], replicated, may hold values from 0.5 to 1.5
- text_second_shift: float32 [512], replicated, may hold values from -3 to 3
- text_widen_weight: bfloat16 [512, 2048], replicated, may hold values from -0.25 to 0.25
- text_narrow_weight: bfloat16 [2048, 512], replicated, may hold values from -0.125 to 0.125
- text_final_gain: float32 [512], replicated, may hold values from 0.5 to 1.5
- text_final_shift: float32 [512], replicated, may hold values from -3 to 3
- text_projection: bfloat16 [512, 512], replicated, may hold values from -0.25 to 0.25
- text_block_out_grad: bfloat16 [1024, 77, 512], P(('tower', 'dp')), may hold values from -0.00024414062 to 0.00024414062
- log_scale: float32 [1], replicated, may hold values from 3.4 to 4.1
Outputs:
- loss: float32 [1], replicated
- image_embedding: bfloat16 [1024, 512], P(('tower', 'dp'))
- text_embedding: bfloat16 [1024, 512], P(('tower', 'dp'))
- image_tokens_grad: float32 [1024, 50, 768], P(('tower', 'dp'))
- image_first_gain_grad: float32 [768], P('dp')
- image_first_shift_grad: float32 [768], P('dp')
- image_joint_weight_grad: float32 [768, 2304], P('dp')
- image_output_weight_grad: float32 [768, 768], P('dp')
- image_second_gain_grad: float32 [768], P('dp')
- image_second_shift_grad: float32 [768], P('dp')
- image_widen_weight_grad: float32 [768, 3072], P('dp')
- image_narrow_weight_grad: float32 [3072, 768], P('dp')
- image_final_gain_grad: float32 [768], P('dp')
- image_final_shift_grad: float32 [768], P('dp')
- image_projection_grad: float32 [768, 512], P('dp')
- text_tokens_grad: float32 [1024, 77, 512], P(('tower', 'dp'))
- text_first_gain_grad: float32 [512], P('dp')
- text_first_shift_grad: float32 [512], P('dp')
- text_joint_weight_grad: float32 [512, 1536], P('dp')
- text_output_weight_grad: float32 [512, 512], P('dp')
- text_second_gain_grad: float32 [512], P('dp')
- text_second_shift_grad: float32 [512], P('dp')
- text_widen_weight_grad: float32 [512, 2048], P('dp')
- text_narrow_weight_grad: float32 [2048, 512], P('dp')
- text_final_gain_grad: float32 [512], P('dp')
- text_final_shift_grad: float32 [512], P('dp')
- text_projection_grad: float32 [512, 512], P('dp')
- log_scale_grad: float32 [1], replicated
Inputs may be any that keep to these rules, and one draw needn't show every extreme that they name: `caption_lengths`: each caption's end-of-text token stands at position length minus 1; some caption has 77 tokens and some has 5.
All inputs are finite; a program needn't handle non-finite values.
Results may differ from a plain program's by a relative error of at most 0.024.
Values may be sent and summed in bfloat16 or wider, within the bound.
No kernel may reach another device: no remote copies, remote signals or barrier semaphores. Data moves between devices by JAX's collectives and lax.ppermute only.
A program may use at most 256 MiB of HBM per device.

v0:
```python
import functools

import jax
import jax.numpy as jnp
from jax import lax
from jax.experimental import pallas as pl
from jax.experimental.pallas import tpu as pltpu
from jax.sharding import PartitionSpec as P

F32 = jnp.float32
BF16 = jnp.bfloat16
BATCH = 8
EMBED = 512
TILE = 256
DEVS = 64


class Tower:
    def __init__(self, width, heads, hidden, length, padded, rows, extra, causal):
        self.width = width
        self.heads = heads
        self.hidden = hidden
        self.length = length
        self.padded = padded
        self.real = BATCH * length
        self.rows = rows
        self.extra = extra
        self.spread = BATCH * padded
        self.lanes = -(-rows // 128) * 128
        self.causal = causal
        self.step = 768 if width == 768 else 512


IMAGE = Tower(768, 12, 3072, 50, 64, 416, 400, False)
TEXT = Tower(512, 8, 2048, 77, 80, 640, 624, True)

VMEM_LIMIT = 64 * 1024 * 1024


def mm(left, right):
    return lax.dot_general(left, right, (((1,), (0,)), ((), ())), preferred_element_type=F32)


def mm_nt(left, right):
    return lax.dot_general(left, right, (((1,), (1,)), ((), ())), preferred_element_type=F32)


def mm_tn(left, right):
    return lax.dot_general(left, right, (((0,), (0,)), ((), ())), preferred_element_type=F32)


def normalise(values):
    centre = jnp.mean(values, axis=-1, keepdims=True)
    offset = values - centre
    inverse = lax.rsqrt(jnp.mean(offset * offset, axis=-1, keepdims=True) + 1e-05)
    return offset * inverse, inverse


def norm_back(upstream, gain, normal, inverse):
    scaled = upstream * gain
    inner = (
        scaled
        - jnp.mean(scaled, axis=-1, keepdims=True)
        - normal * jnp.mean(scaled * normal, axis=-1, keepdims=True)
    )
    return inner * inverse


def column_sum(values):
    return jnp.sum(values, axis=0, keepdims=True)


def sigmoid(values):
    return 0.5 + 0.5 * jnp.tanh(0.5 * values)


def vec(ref):
    return ref[...].reshape(1, -1)


def chunks(count, size=128):
    return [(at, min(size, count - at)) for at in range(0, count, size)]


UNROLL_TILE, UNROLL_HEADS, UNROLL_PACK = 9, 8, 4
UNROLL_BACK = 1


def loop(count, body, unroll=1):
    def step(i, carry):
        body(i)
        return carry

    lax.fori_loop(0, count, step, 0, unroll=min(unroll, count))


def tile_loop(width, body):
    loop(width // TILE, lambda n: body(n, pl.ds(pl.multiple_of(n * TILE, TILE), TILE)), UNROLL_TILE)


def put_tiles(ref, n, rows, values):
    for i in range(TILE // 128):
        ref[n * (TILE // 128) + i, 0:rows, :] = values[:, 128 * i : 128 * i + 128]


class Lazy:
    def __init__(self, queue, source, target, sem):
        self.copy = pltpu.make_async_copy(source, target, sem)
        self.target = target
        self.queue = queue
        self.started = self.waited = False

    def start(self):
        if not self.started:
            self.copy.start()
            self.started = True

    def get(self):
        if not self.waited:
            self.start()
            self.copy.wait()
            self.waited = True
            for item in self.queue:
                if not item.started:
                    item.start()
                    break
        return self.target


class Staged:
    def __init__(self, out, stage, sems, pending):
        self.out = out
        self.ref = stage
        self.sems = sems
        self.pending = pending

    def send(self, source, target):
        copy = pltpu.make_async_copy(source, target, self.sems.at[len(self.pending)])
        copy.start()
        self.pending.append(copy)

    def done(self):
        self.send(self.ref, self.out)

    def units_done(self, devices, units, out_units):
        self.send(self.ref.at[devices, units], self.out.at[devices, out_units])


def head_masks():
    lane = lax.broadcasted_iota(jnp.int32, (1, 128), 1)
    first = jnp.where(lane < 64, 1.0, 0.0).astype(BF16)
    second = jnp.where(lane < 64, 0.0, 1.0).astype(BF16)
    return first, second


def two_heads(values, masks):
    return jnp.concatenate([values * masks[0], values * masks[1]], axis=0)


def own_head(values, padded):
    lane = lax.broadcasted_iota(jnp.int32, (padded, 128), 1)
    return jnp.where(lane < 64, values[:padded], values[padded:])


def pooled_row(t, lengths, b):
    return b if t is IMAGE else (lengths[b] - 1) * BATCH + b


def row_parts(t):
    return {
        "raw": EMBED,
        "unit": EMBED,
        "pooled": t.width,
        "mixed": t.width,
        "grad": t.width,
        "wide": t.hidden,
    }


def row_part(t, name):
    at = 0 if t is IMAGE else sum(row_parts(IMAGE).values())
    for part, size in row_parts(t).items():
        if part == name:
            return slice(at, at + size)
        at += size


ROW_TOTAL = sum(row_parts(IMAGE).values()) + sum(row_parts(TEXT).values())


class Front:
    def __init__(self, t, lengths, ins, weights, outs, kept, scratch):
        self.t = t
        self.lengths = lengths
        (
            self.tokens,
            self.first_gain,
            self.first_shift,
            self.second_gain,
            self.second_shift,
            self.final_gain,
            self.final_shift,
            self.block_grad,
        ) = ins
        self.joint_weight, self.output_weight, self.widen, self.narrow, self.projection = weights
        self.staged = outs[:4]
        self.turned, self.joint, self.probs, self.mixed = [out.ref for out in outs[:4]]
        self.unit = outs[4]
        self.kept = kept
        self.joint_wide, self.context_wide, self.normed_one, self.context = scratch
        self.mixed_row = kept.at[:, row_part(t, "mixed")]

    def norm(self):
        t, rows = self.t, self.t.rows
        mixed, normed_one = self.mixed, self.normed_one
        grad_row = self.kept.at[:, row_part(t, "grad")]
        for at, size in chunks(t.real):
            mixed[at : at + size, :] = self.block_grad[at : at + size, :].astype(F32)
        for b in range(BATCH):
            grad_row[b : b + 1, :] = mixed[pl.ds(pooled_row(t, self.lengths, b), 1), :]
        pad = t.real - t.real % 16
        normed_one[pad:rows, :] = jnp.zeros((rows - pad, t.width), BF16)
        for at, size in chunks(t.real):
            normal, _ = normalise(self.tokens[at : at + size, :].astype(F32))
            normed_one[at : at + size, :] = (
                normal * vec(self.first_gain) + vec(self.first_shift)
            ).astype(BF16)
        if t.spread > rows:
            fill = (3 * t.width // 128, t.spread - rows, 128)
            self.joint_wide[:, rows : t.spread, :] = jnp.zeros(fill, F32)

    def joint_tile(self, n):
        cols = pl.ds(pl.multiple_of(n * TILE, TILE), TILE)
        product = mm(self.normed_one[...], self.joint_weight.get()[:, cols])
        put_tiles(self.joint_wide, n, self.t.rows, product)

    def ready(self):
        t, padded = self.t, self.t.padded
        self.masks = head_masks()
        key_at = lax.broadcasted_iota(jnp.int32, (padded, 2 * padded), 0)
        query_at = lax.broadcasted_iota(jnp.int32, (padded, 2 * padded), 1)
        query_at = jnp.where(query_at < padded, query_at, query_at - padded)
        self.valid = key_at <= query_at if t.causal else key_at < t.length

    def attend(self, b):
        t, joint, masks = self.t, self.joint, self.masks
        width, padded = t.width, t.padded
        pairs = range(t.heads // 2)
        some = pl.ds(b, padded, stride=BATCH)
        for c in range(3 * width // 128):
            joint[b, :, 128 * c : 128 * c + 128] = self.joint_wide[c, some, :].astype(BF16)
        scores = []
        for p in pairs:
            at = 128 * p
            queries = joint[b, :, at : at + 128]
            keys = joint[b, :, width + at : width + at + 128]
            scores.append(mm_nt(keys, two_heads(queries, masks)) * 0.125)
        lows = []
        for p in pairs:
            score = jnp.where(self.valid, scores[p], -1e30)
            raised = jnp.exp(score - jnp.max(score, axis=0, keepdims=True))
            low = (raised * (1.0 / column_sum(raised))).astype(BF16)
            self.probs[b, p] = low
            lows.append(low)
        for p in pairs:
            at = 2 * width + 128 * p
            both = mm_tn(lows[p], joint[b, :, at : at + 128])
            self.context_wide[p, some, :] = own_head(both, padded)

    def mix(self):
        t, rows, width = self.t, self.t.rows, self.t.width
        context, mixed = self.context, self.mixed
        self.staged[1].done()
        self.staged[2].done()
        for p in range(t.heads // 2):
            context[:, 128 * p : 128 * p + 128] = self.context_wide[p, 0:rows, :].astype(BF16)
        turn(self.normed_one, self.turned.at[0:width], 6)
        turn(context, self.turned.at[width : 2 * width], 6)
        self.staged[0].done()
        output_weight = self.output_weight.get()

        def mix_step(n, cols):
            mixed[:, cols] = mm(context[...], output_weight[:, cols])

        tile_loop(width, mix_step)
        for at, size in chunks(t.real):
            mixed[at : at + size, :] += self.tokens[at : at + size, :].astype(F32)
        for b in range(BATCH):
            row = mixed[pl.ds(pooled_row(t, self.lengths, b), 1), :]
            self.mixed_row[b : b + 1, :] = row
        mixed[t.real : rows, :] = jnp.zeros((rows - t.real, width), F32)
        mixed[t.extra : t.extra + BATCH, :] = self.mixed_row[...]
        self.staged[3].done()

    def embed(self):
        t, kept = self.t, self.kept
        row = self.mixed_row[...]
        normal, _ = normalise(row)
        normed = (normal * vec(self.second_gain) + vec(self.second_shift)).astype(BF16)
        wide = mm(normed, self.widen.get()[...])
        kept[:, row_part(t, "wide")] = wide
        active = (wide * sigmoid(1.702 * wide)).astype(BF16)
        last = row + mm(active, self.narrow.get()[...])
        kept[:, row_part(t, "pooled")] = last
        normal, _ = normalise(last)
        normed = (normal * vec(self.final_gain) + vec(self.final_shift)).astype(BF16)
        raw = mm(normed, self.projection.get()[...])
        kept[:, row_part(t, "raw")] = raw
        factor = lax.rsqrt(jnp.sum(raw * raw, axis=-1, keepdims=True) + 1e-06)
        unit = (raw * factor).astype(BF16)
        self.unit[...] = unit
        kept[:, row_part(t, "unit")] = unit.astype(F32)
        return unit


def fronts_kernel(scalars, held, lazies, outs, scratch):
    order = [5, 6, 0, 7, 8, 9, 1, 2, 3, 4]
    weights = [lazies[order.index(i)] for i in range(10)]
    image, text = [
        Front(
            t,
            scalars[0],
            held[8 * i : 8 * i + 8],
            weights[5 * i : 5 * i + 5],
            outs[5 * i : 5 * i + 5],
            outs[10],
            scratch[4 * i : 4 * i + 4],
        )
        for i, t in enumerate((IMAGE, TEXT))
    ]
    text.norm()
    for n in range(3 * TEXT.width // TILE):
        text.joint_tile(n)
    image.norm()
    for front in (image, text):
        front.ready()
    image.joint_weight.get()
    tiles = 3 * IMAGE.width // TILE

    def both(b):
        text.attend(b)
        image.joint_tile(b)

    loop(BATCH, both, UNROLL_HEADS)
    for n in range(BATCH, tiles):
        image.joint_tile(n)
    text.mix()
    loop(BATCH, image.attend, UNROLL_HEADS)
    image.mix()
    for i, unit in enumerate((image.embed(), text.embed())):
        outs[11][:, :, EMBED * i : EMBED * i + EMBED] = jnp.broadcast_to(unit[None], (DEVS, *unit.shape))


def middle_kernel(
    t,
    place,
    lengths,
    mixed,
    block_grad,
    second_gain,
    second_shift,
    widen_weight,
    narrow_weight,
    normed_turned,
    active_turned,
    wide_own,
    wide_send,
    narrow_own,
    narrow_send,
    mixed_grad,
    gain_grad,
    shift_grad,
    normed_two,
    narrow_in,
    wide_in,
):
    step = pl.program_id(0)
    half_steps = pl.num_programs(0) // 2

    @pl.when(step == 0)
    def _():
        wide_in[t.real : t.rows, :] = jnp.zeros((t.rows - t.real, t.width), F32)
        for at, size in chunks(t.rows):
            normal, _ = normalise(mixed[at : at + size, :])
            normed_two[at : at + size, :] = (normal * vec(second_gain) + vec(second_shift)).astype(
                BF16
            )
        turn(normed_two, normed_turned)
        for at, size in chunks(t.real):
            wide_in[at : at + size, :] = block_grad[at : at + size, :].astype(F32)
        for b in range(BATCH):
            wide_in[pl.ds(pooled_row(t, lengths, b), 1), :] = jnp.zeros((1, t.width), F32)
        narrow_in[...] = wide_in[...].astype(BF16)
        cols = t.width // 2
        own = pl.multiple_of(place[0] * cols, 128)
        narrow_own[...] = narrow_in[:, pl.ds(own, cols)]
        narrow_send[...] = narrow_in[:, pl.ds(pl.multiple_of(cols - own, 128), cols)]
        mixed_grad[...] = jnp.zeros_like(mixed_grad)

    lows = []
    for at, size in chunks(t.step, TILE):
        some = slice(at, at + size)
        wide = mm(normed_two[...], widen_weight[:, some])
        back = mm_nt(narrow_in[...], narrow_weight[some, :])
        sig = sigmoid(1.702 * wide)
        active = wide * sig
        active_turned[some, 0 : t.rows] = active.astype(BF16).T
        slope = sig + 1.702 * active * (1.0 - sig)
        lows.append((back * slope).astype(BF16))
    low = jnp.concatenate(lows, axis=1)
    mixed_grad[...] += mm_nt(low, widen_weight[...])

    @pl.when(step < half_steps)
    def _():
        wide_own[...] = low

    @pl.when(step >= half_steps)
    def _():
        wide_send[...] = low

    @pl.when(step == pl.num_programs(0) - 1)
    def _():
        gain = shift = 0.0
        for at, size in chunks(t.rows):
            some = slice(at, at + size)
            normal, inverse = normalise(mixed[some, :])
            up = mixed_grad[some, :]
            gain += column_sum(up * normal)
            shift += column_sum(up)
            mixed_grad[some, :] = wide_in[some, :] + norm_back(
                up, vec(second_gain), normal, inverse
            )
        gain_grad[...] = gain
        shift_grad[...] = shift


def split_dot(weights, right):
    high = weights.astype(BF16)
    rest = weights - high.astype(F32)
    middle = rest.astype(BF16)
    low = (rest - middle.astype(F32)).astype(BF16)
    return mm(high, right) + mm(middle, right) + mm(low, right)


def head_back(
    unit_grad,
    raw,
    pooled,
    mixed_row,
    wide_row,
    grad_row,
    final_gain,
    final_shift,
    second_gain,
    second_shift,
    projection,
    widen_weight,
    narrow_weight,
    outs,
):
    (
        final_gain_grad,
        final_shift_grad,
        second_gain_grad,
        second_shift_grad,
        factors,
        mixed_grad_row,
        narrow_in_row,
        wide_grad_row,
    ) = outs
    own = slice(0, BATCH)
    width = pooled.shape[1]
    factor = lax.rsqrt(jnp.sum(raw * raw, axis=-1, keepdims=True) + 1e-06)
    raw_grad = factor * unit_grad - raw * (factor * factor * factor) * jnp.sum(
        unit_grad * raw, axis=-1, keepdims=True
    )
    raw_grad = raw_grad.astype(BF16)
    factors[:, width:] = raw_grad.astype(F32)
    normal, inverse = normalise(pooled)
    factors[:, 0:width] = (normal * final_gain + final_shift).astype(BF16).astype(F32)
    up = mm_nt(raw_grad, projection.get()[...])
    final_gain_grad[...] = column_sum((up * normal)[own])
    final_shift_grad[...] = column_sum(up[own])
    out_grad = grad_row + norm_back(up, final_gain, normal, inverse)
    narrow_in = out_grad.astype(BF16)
    narrow_in_row[...] = narrow_in.astype(F32)
    sig = sigmoid(1.702 * wide_row)
    slope = sig + 1.702 * wide_row * sig * (1.0 - sig)
    low = (mm_nt(narrow_in, narrow_weight.get()[...]) * slope).astype(BF16)
    wide_grad_row[...] = low.astype(F32)
    up = mm_nt(low, widen_weight.get()[...])
    normal, inverse = normalise(mixed_row)
    second_gain_grad[...] = column_sum((up * normal)[own])
    second_shift_grad[...] = column_sum(up[own])
    mixed_grad_row[...] = (out_grad + norm_back(up, second_gain, normal, inverse))[own]


def kept_rows(own, other, t, name):
    some = row_part(t, name)
    return jnp.concatenate([own[:, some], other[:, some]], axis=0)


def head_of(t, unit_grad, kept, vectors, weights, outs):
    values = [kept_rows(*kept, t, name) for name in ("raw", "pooled", "mixed", "wide", "grad")]
    values += [vec(ref) for ref in vectors]
    projection, narrow, widen = weights
    head_back(unit_grad, *values, projection, widen, narrow, outs)


def pair_kernel(scalars, held, lazies, outs, scratch):
    place, log_scale = scalars
    own, other, kept_own, kept_other = held[:4]
    loss, scale_grad, text_grad = outs[:3]
    kept = (kept_own, kept_other)
    half = own.shape[0]
    pairs = 2 * half
    scale = jnp.exp(jnp.full((1, 1), log_scale[0], F32))
    blocks = (own, other)

    def totals(left_at, right_at):
        sums, moments = [], []
        for right in blocks:
            column, moment = None, None
            for left in blocks:
                for piece in range(0, half, 256):
                    sims = scale * mm_nt(
                        left[piece : piece + 256, left_at : left_at + EMBED],
                        right[:, right_at : right_at + EMBED],
                    )
                    raised = jnp.exp(sims)
                    add, more = column_sum(raised), column_sum(raised * sims)
                    column = add if column is None else column + add
                    moment = more if moment is None else moment + more
            sums.append(column)
            moments.append(moment)
        return sums, moments

    column_sums, column_moments = totals(0, EMBED)
    row_sums, row_moments = totals(EMBED, 0)
    log_total = jnp.zeros((1, 1), F32)
    weighted = jnp.zeros((1, 1), F32)
    trace = jnp.zeros((1, 1), F32)
    for i in range(2):
        for total, moment in ((column_sums[i], column_moments[i]), (row_sums[i], row_moments[i])):
            log_total += jnp.sum(jnp.log(total), axis=-1, keepdims=True)
            weighted += jnp.sum(moment / total, axis=-1, keepdims=True)
        product = blocks[i][:, :EMBED].astype(F32) * blocks[i][:, EMBED:].astype(F32)
        trace += jnp.sum(column_sum(product), axis=-1, keepdims=True)
    trace = scale * trace
    loss[...] = jnp.broadcast_to((log_total - 2.0 * trace) / (2.0 * pairs), loss.shape)
    scale_grad[...] = jnp.broadcast_to((weighted - 2.0 * trace) / (2.0 * pairs), loss.shape)

    lane = lax.broadcasted_iota(jnp.int32, (2 * BATCH, half), 1)
    sub = lax.broadcasted_iota(jnp.int32, (2 * BATCH, half), 0)
    diagonal = place[1] * BATCH
    identity = [
        jnp.where(jnp.logical_and(lane == sub + diagonal, sub < BATCH), 2.0, 0.0),
        jnp.where(jnp.logical_and(lane == sub - BATCH + diagonal, sub >= BATCH), 2.0, 0.0),
    ]

    def grads(t, at, other_sums):
        unit = kept_rows(*kept, t, "unit").astype(BF16)
        raised = [jnp.exp(scale * mm_nt(unit, block[:, at : at + EMBED])) for block in blocks]
        own_sum = sum(jnp.sum(r, axis=-1, keepdims=True) for r in raised)
        result = None
        for i in range(2):
            weight = raised[i] * (1.0 / own_sum + 1.0 / other_sums[i]) - identity[i]
            weight = weight / (2.0 * pairs)
            part = split_dot(weight, blocks[i][:, at : at + EMBED])
            result = part if result is None else result + part
        return scale * result

    image_grad = grads(IMAGE, EMBED, column_sums)
    text_grad[...] = grads(TEXT, 0, row_sums)
    head_of(IMAGE, image_grad, kept, held[4:8], lazies, outs[3:11])


class Back:
    def __init__(self, t, place, lengths, held, lazies, outs, scratch):
        self.t = t
        self.place = place
        self.lengths = lengths
        self.tokens, self.first_gain, self.row = held[:3]
        self.output_weight, self.mixed_grad, self.joint_in, self.probs_in, self.joint_weight = lazies
        self.own, self.send, self.tokens_out, self.gain_grad, self.shift_grad = outs
        self.context_grad, self.joint_grad, self.normed_grad, self.grads = scratch

    def context(self):
        t, rows, width, grads = self.t, self.t.rows, self.t.width, self.grads
        self.grad = grad = self.mixed_grad.get()
        for b in range(BATCH):
            grad[pl.ds(pooled_row(t, self.lengths, b), 1), :] = self.row[b : b + 1, :]
        mixed_low = slice(3 * width, 4 * width)
        grads[:, mixed_low] = grad[...].astype(BF16)
        if t.spread > rows:
            fill = (width // 128, t.spread - rows, 128)
            self.context_grad[:, rows : t.spread, :] = jnp.zeros(fill, F32)
        output_weight = self.output_weight.get()

        def step(n, cols):
            put_tiles(self.context_grad, n, rows, mm_nt(grads[:, mixed_low], output_weight[cols, :]))

        tile_loop(width, step)
        self.masks = head_masks()
        self.joint, self.probs = self.joint_in.get(), self.probs_in.get()

    def attend(self, b):
        t, masks, joint, joint_grad = self.t, self.masks, self.joint, self.joint_grad
        width, padded = t.width, t.padded
        pairs = range(t.heads // 2)
        some = pl.ds(b, padded, stride=BATCH)
        ups = [two_heads(self.context_grad[p, some, :].astype(BF16), masks) for p in pairs]
        backs = []
        for p in pairs:
            at = 2 * width + 128 * p
            backs.append(mm_nt(joint[b, :, at : at + 128], ups[p]))
        lows = []
        for p in pairs:
            wide = self.probs[b, p].astype(F32)
            back = wide * (backs[p] - column_sum(backs[p] * wide))
            lows.append(back.astype(BF16))
        for p in pairs:
            at = 128 * p
            queries = joint[b, :, at : at + 128]
            keys = joint[b, :, width + at : width + at + 128]
            joint_grad[2 * len(pairs) + p, some, :] = mm(self.probs[b, p], ups[p])
            joint_grad[len(pairs) + p, some, :] = mm(lows[p], two_heads(queries, masks)) * 0.125
            joint_grad[p, some, :] = own_head(mm_tn(lows[p], keys), padded) * 0.125

    def finish(self):
        t, rows, width, grads = self.t, self.t.rows, self.t.width, self.grads
        for c in range(3 * width // 128):
            grads[:, 128 * c : 128 * c + 128] = self.joint_grad[c, 0:rows, :].astype(BF16)
        start = pl.multiple_of(self.place[0] * (2 * width), 128)
        self.own.send(grads.at[:, pl.ds(start, 2 * width)], self.own.out)
        start = pl.multiple_of(2 * width - start, 128)
        self.send.send(grads.at[:, pl.ds(start, 2 * width)], self.send.out)
        joint_weight = self.joint_weight.get()

        def step(n, cols):
            self.normed_grad[:, cols] = mm_nt(grads[:, 0 : 3 * width], joint_weight[cols, :])

        tile_loop(width, step)
        gain = shift = 0.0
        for at, size in chunks(t.real):
            some = slice(at, at + size)
            normal, inverse = normalise(self.tokens[some, :].astype(F32))
            up = self.normed_grad[some, :]
            gain += column_sum(up * normal)
            shift += column_sum(up)
            self.tokens_out.ref[some, :] = self.grad[some, :] + norm_back(
                up, vec(self.first_gain), normal, inverse
            )
        self.gain_grad[...] = gain
        self.shift_grad[...] = shift
        self.tokens_out.done()


def backs_kernel(scalars, held, lazies, outs, scratch):
    head_in, held = held[:7], held[7:]
    head_weights, lazies = lazies[:3], lazies[3:]
    head_outs, outs = outs[:8], outs[8:]
    head_of(TEXT, head_in[0][...], head_in[1:3], head_in[3:7], head_weights, head_outs)
    order = [5, 6, 0, 1, 7, 8, 2, 3, 9, 4]
    lazies = [lazies[order.index(i)] for i in range(10)]
    held = [*held[:3], *held[3:5], head_outs[5]]
    image, text = [
        Back(
            t,
            *scalars,
            held[3 * i : 3 * i + 3],
            lazies[5 * i : 5 * i + 5],
            outs[5 * i : 5 * i + 5],
            scratch[4 * i : 4 * i + 4],
        )
        for i, t in enumerate((IMAGE, TEXT))
    ]
    text.context()
    image.context()

    def both(b):
        text.attend(b)
        image.attend(b)

    loop(BATCH, both, UNROLL_BACK)
    text.finish()
    image.finish()


def turn(source, target, unroll=3):
    def step(n):
        cols = pl.ds(pl.multiple_of(n * 128, 128), 128)
        target[cols, 0 : source.shape[0]] = source[:, cols].T

    loop(source.shape[1] // 128, step, unroll)


def lanes_down(values):
    return jnp.concatenate(
        [values[:, :, at : at + 128] for at in range(0, values.shape[2], 128)], axis=1
    )


def put(out, device, unit, values):
    count = values.shape[1] // 16
    size = values.shape[0]
    values = values.reshape(size, count, 16, 128).astype(BF16)
    out[pl.ds(device, size), unit : unit + count] = values


def pack_twelve(first, second, out, unit=0, each=4):
    cols = first.shape[1]
    count = cols // 128
    sub = lax.broadcasted_iota(jnp.int32, (each, 8, cols), 1) < 4

    def step(e):
        rows = pl.ds(pl.multiple_of(e * (24 * each), 8), 24 * each)
        x = first[rows, :].reshape(each, 24, cols)
        y = second[rows, :].reshape(each, 24, cols)
        left, right = x[:, 8:16], y[:, 8:16]
        even = jnp.where(sub, left, pltpu.roll(right, 4, 1))
        odd = jnp.where(sub, pltpu.roll(left, 4, 1), right)
        parts = []
        for a, b, c in ((x[:, 0:8], y[:, 0:8], even), (x[:, 16:24], y[:, 16:24], odd)):
            parts.append(jnp.concatenate([lanes_down(v) for v in (a, b, c)], axis=1))
        if parts[0].shape[1] % 16:
            fill = jnp.zeros((each, 16 - parts[0].shape[1] % 16, 128), F32)
            parts = [jnp.concatenate([part, fill], axis=1) for part in parts]
        height = parts[0].shape[1]
        values = jnp.stack(parts, axis=1).reshape(2 * each, height, 128)
        put(out, e * (2 * each), unit, values)

    loop(32 // each, step, UNROLL_PACK)


def pack_rows(result, rows, out, unit=0, each=8, device=0):
    total = result.shape[0] // rows
    cols = result.shape[1]

    def step(e):
        some = pl.ds(pl.multiple_of(e * (rows * each), 8), rows * each)
        values = lanes_down(result[some, :].reshape(each, rows, cols))
        put(out, device + e * each, unit, values)

    loop(total // each, step, UNROLL_PACK)


def put_extra(t, ref, rows):
    rows = jnp.concatenate([rows, jnp.zeros_like(rows)], axis=0)
    ref[t.extra : t.extra + 16, :] = rows.astype(BF16)


def wide_grads(t, half, product, send, at, first, second):
    if t is IMAGE:
        for i in range(3):
            first[...] = product(256 * i, 256)
            second[...] = product(768 + 256 * i, 256)
            pack_twelve(first, second, send.ref, 3 * i)
            units = slice(3 * i, 3 * i + 3)
            send.units_done(slice(None), units, slice(at + 3 * i, at + 3 * i + 3))
    else:
        for i in range(2):
            first[...] = product(512 * i, 512)
            pack_rows(first, 8, send.ref, 2 * i)
            units = slice(2 * i, 2 * i + 2)
            send.units_done(slice(None), units, slice(at + 2 * i, at + 2 * i + 2))


def feed_kernel(t, at, scalars, held, lazies, outs, scratch):
    (place,) = scalars
    wide_rows, narrow_rows = held
    normed, wides, narrows = lazies[0:2], lazies[2:4], lazies[4:6]
    actives = lazies[6:14]
    (out,) = outs
    first, second, narrow_result = scratch

    def patch(refs, rows):
        size = rows.shape[1] // 2
        some = pl.ds(pl.multiple_of(place[0] * size, 128), size)
        for side, ref in enumerate(refs):
            put_extra(t, ref.get(), rows[BATCH * side : BATCH * side + BATCH, some])

    patch(wides, wide_rows)
    lefts = [ref.get() for ref in normed]
    wides = [ref.get() for ref in wides]

    def product(tile, size):
        return sum(mm(a[:, 0 : t.rows], b[:, tile : tile + size]) for a, b in zip(lefts, wides))

    wide_grads(t, place[0], product, out, at, first, second)
    patch(narrows, narrow_rows)
    narrows = [ref.get() for ref in narrows]
    wide_units, units = (9, 9) if t is IMAGE else (4, 4)
    some = slice(wide_units, wide_units + units)
    for j in range(4):
        pair = [actives[2 * j].get(), actives[2 * j + 1].get()]
        narrow_result[...] = sum(mm(a[:, 0 : t.rows], b[...]) for a, b in zip(pair, narrows))
        pack_rows(narrow_result, t.hidden // DEVS, out.ref, wide_units, 4, 16 * j)
        out.units_done(
            slice(16 * j, 16 * j + 16), some, slice(at + wide_units, at + wide_units + units)
        )


def rest_kernel(scalars, held, lazies, outs, scratch):
    (place,) = scalars
    (out,) = outs
    first, second, third = scratch[:3]
    misc_scratch, spread = scratch[3:6], scratch[6]
    half = place[0]
    misc, text_stage, image_stage = [Staged(out.out, ref, out.sems, out.pending) for ref in scratch[7:10]]
    misc_grads(half, held[:2], held[2:], misc, misc_scratch, spread)
    for t, ins, stage, results in (
        (TEXT, lazies[0:4], text_stage, (third, None)),
        (IMAGE, lazies[4:8], image_stage, (first, second)),
    ):
        width = t.width
        lefts, rights = [ref.get() for ref in ins[0::2]], [ref.get() for ref in ins[1::2]]

        def product(tile, size):
            late = jnp.where(half * (2 * width) + tile >= 3 * width, width, 0)
            rows = pl.ds(pl.multiple_of(late, 128), width)
            return sum(
                mm(a[rows, 0 : t.rows], b[:, tile : tile + size]) for a, b in zip(lefts, rights)
            )

        wide_grads(t, half, product, stage, REST_AT["image" if t is IMAGE else "text"], *results)


IMAGE_FEED_UNITS = 18
LATE_UNITS = 24
TEXT_FEED_AT = 0
REST_AT = {"text": 8, "image": 15}
MISC_AT = 12


def misc_grads(half, factors, vectors, out, scratch, spread):
    image_factors, text_factors = factors
    first, second, third = scratch

    def product(t, ref, at, size):
        final = ref[:, 0 : t.width].astype(BF16)
        start = pl.multiple_of(t.width + half * 256 + at, 128)
        return mm_tn(final, ref[:, pl.ds(start, size)].astype(BF16))

    first[...] = product(IMAGE, image_factors, 0, 128)
    second[...] = product(IMAGE, image_factors, 128, 128)
    third[...] = product(TEXT, text_factors, 0, 256)
    pack_twelve(first, second, out.ref, 1, 8)
    pack_rows(third, 8, out.ref, 0)
    spread[...] = jnp.zeros_like(spread)
    for side, refs_of, width in ((0, vectors[:8], 768), (64, vectors[8:], 512)):
        each = width // DEVS
        device = lax.broadcasted_iota(jnp.int32, (DEVS, width), 0)
        column = lax.broadcasted_iota(jnp.int32, (DEVS, width), 1)
        mine = jnp.logical_and(column >= device * each, column < device * each + each)
        source = lax.broadcasted_iota(jnp.int32, (width, 128), 0)
        lane = lax.broadcasted_iota(jnp.int32, (width, 128), 1)
        at = lax.rem(source, each)
        high_at = jnp.where(lane == at + side, 1.0, 0.0).astype(BF16)
        low_at = jnp.where(lane == at + side + 32, 1.0, 0.0).astype(BF16)
        rows = [refs_of[0][...], refs_of[1][...], refs_of[2][...] + refs_of[3][...]]
        rows += [refs_of[4][...] + refs_of[5][...], refs_of[6][...], refs_of[7][...]]
        for k, row in enumerate(rows):
            row = jnp.where(mine, row, 0.0)
            high = row.astype(BF16)
            low = (row - high.astype(F32)).astype(BF16)
            spread[:, 8 + k, :] += mm(high, high_at) + mm(low, low_at)
    out.ref[:, 2] = (out.ref[:, 2].astype(F32) + spread[...]).astype(BF16)
    out.units_done(slice(None), slice(0, 3), slice(MISC_AT, MISC_AT + 3))


def unpack_kernel(place, mine, other, *outs):
    split = 16 * IMAGE_FEED_UNITS
    feed_mine, feed_other = mine.at[0:split], other.at[0:split]
    late_mine, late_other = mine.at[split:], other.at[split:]
    (
        image_joint,
        image_output,
        image_widen,
        image_narrow,
        image_projection,
        text_joint,
        text_output,
        text_widen,
        text_narrow,
        text_projection,
    ) = outs[:10]
    odd = place[1] % 2

    def emit(half, feed, late):
        def into(ref, col, body, tail):
            @pl.when(odd == 0)
            def _():
                ref[0:8, col : col + 128] = body
                ref[8:12, col : col + 128] = tail

            @pl.when(odd == 1)
            def _():
                ref[0:4, col : col + 128] = tail
                ref[4:12, col : col + 128] = body

        def image_wide(source, at, store):
            for tile in range(3):
                block = source[16 * (at + 3 * tile) : 16 * (at + 3 * tile) + 48, :]
                for side in range(2):
                    for g in range(2):
                        body = block[16 * side + 8 * g : 16 * side + 8 * g + 8]
                        tail = block[32 + 8 * g + 4 * side : 36 + 8 * g + 4 * side]
                        store(half * 1536 + side * 768 + tile * 256 + g * 128, body, tail)

        def joint_store(col, body, tail):
            if col < 2304:
                into(image_joint, col, body, tail)
            else:
                into(image_output, col - 2304, body, tail)

        image_wide(feed, 0, functools.partial(into, image_widen))
        image_wide(late, REST_AT["image"], joint_store)
        at = 16 * 9
        for g in range(3):
            col = half * 384 + 128 * g
            image_narrow[:, col : col + 128] = feed[at + 48 * g : at + 48 * g + 48, :]
        at = 16 * (MISC_AT + 1)
        for side in range(2):
            col = half * 256 + 128 * side
            tail = late[at + 16 + 4 * side : at + 20 + 4 * side, :]
            into(image_projection, col, late[at + 8 * side : at + 8 * side + 8, :], tail)
        for g in range(8):
            col = half * 1024 + 128 * g
            at = 16 * TEXT_FEED_AT + 8 * g
            text_widen[:, col : col + 128] = late[at : at + 8, :]
            at = 16 * REST_AT["text"] + 8 * g
            block = late[at : at + 8, :]
            if col < 1536:
                text_joint[:, col : col + 128] = block
            else:
                text_output[:, col - 1536 : col - 1408] = block
        for g in range(2):
            col = half * 256 + 128 * g
            at = 16 * (TEXT_FEED_AT + 4) + 32 * g
            text_narrow[:, col : col + 128] = late[at : at + 32, :]
            at = 16 * MISC_AT + 8 * g
            text_projection[:, col : col + 128] = late[at : at + 8, :]

    for half in range(2):

        @pl.when(place[0] == half)
        def _():
            emit(half, feed_mine, late_mine)
            emit(1 - half, feed_other, late_other)

    at = 16 * (MISC_AT + 2) + 8
    vectors = late_mine[at : at + 8, :] + late_other[at : at + 8, :]
    for k in range(12):
        each, side = (12, 0) if k < 6 else (8, 64)
        row = vectors[k % 6 : k % 6 + 1, :]
        outs[10 + k][...] = row[:, side : side + each] + row[:, side + 32 : side + 32 + each]


SMEM = pl.BlockSpec(memory_space=pltpu.SMEM)
VMEM = pl.BlockSpec(memory_space=pltpu.VMEM)


def call(body, name, scalars, arrays, outs, scratch=(), flops=1 << 32):
    return pl.pallas_call(
        body,
        name=name,
        out_shape=tuple(jax.ShapeDtypeStruct(shape, kind) for shape, kind in outs),
        in_specs=[SMEM] * len(scalars) + [VMEM] * len(arrays),
        out_specs=tuple(VMEM for _ in outs),
        scratch_shapes=[pltpu.VMEM(shape, kind) for shape, kind in scratch],
        compiler_params=pltpu.CompilerParams(vmem_limit_bytes=VMEM_LIMIT),
        cost_estimate=pl.CostEstimate(flops=flops, bytes_accessed=20 << 20, transcendentals=0),
    )(*scalars, *arrays)


BIG = 1 << 18


def lazy_call(body, name, scalars, held, lazies, outs, scratch=(), flops=1 << 33, buffer=None, after=(), ahead=3):
    many = 24

    def kernel(*refs):
        refs = list(refs)

        def take(count):
            got = refs[:count]
            del refs[:count]
            return got

        scalar_refs, held_refs = take(len(scalars)), take(len(held))
        sources = take(len(lazies))
        take(len(after) + (buffer is not None))
        out_refs = take(len(outs))
        targets = take(len(lazies))
        stages = take(sum(1 for out in outs if out[2]))
        scratch_refs = take(len(scratch))
        in_sems, out_sems = refs
        lazy = []
        for i, (source, target, (_, index, _)) in enumerate(zip(sources, targets, lazies)):
            if index is not None:
                source = source.at[index(*scalar_refs)]
            lazy.append(Lazy(lazy, source, target, in_sems.at[i]))
        for item in lazy[:ahead]:
            item.start()
        pending = []
        results = []
        for out, ref in zip(outs, out_refs):
            if out[2] is None:
                results.append(ref)
            else:
                results.append(Staged(ref, stages.pop(0) if out[2] else None, out_sems, pending))
        body(scalar_refs, held_refs, lazy, results, scratch_refs)
        for item in lazy:
            if item.started:
                item.get()
        for copy in pending:
            copy.wait()

    any_spec = pl.BlockSpec(memory_space=pl.ANY)
    scratch_shapes = [pltpu.VMEM(shape, array.dtype) for array, _, shape in lazies]
    scratch_shapes += [pltpu.VMEM(stage, kind) for _, kind, stage in outs if stage]
    scratch_shapes += [pltpu.VMEM(shape, kind) for shape, kind in scratch]
    scratch_shapes += [pltpu.SemaphoreType.DMA((max(1, len(lazies)),)), pltpu.SemaphoreType.DMA((many,))]
    arrays = [*held, *[array for array, _, _ in lazies], *after]
    specs = [SMEM] * len(scalars) + [VMEM] * len(held) + [any_spec] * (len(lazies) + len(after))
    aliases = {}
    if buffer is not None:
        aliases = {len(scalars) + len(arrays): 0}
        arrays.append(buffer)
        specs.append(any_spec)
    return pl.pallas_call(
        kernel,
        name=name,
        out_shape=tuple(jax.ShapeDtypeStruct(shape, kind) for shape, kind, _ in outs),
        in_specs=specs,
        out_specs=tuple(VMEM if stage is None else any_spec for _, _, stage in outs),
        scratch_shapes=scratch_shapes,
        input_output_aliases=aliases,
        compiler_params=pltpu.CompilerParams(vmem_limit_bytes=VMEM_LIMIT),
        cost_estimate=pl.CostEstimate(flops=flops, bytes_accessed=20 << 20, transcendentals=0),
    )(*scalars, *arrays)


def all_of(array):
    return array, None, array.shape


def staged(shape, kind):
    return shape, kind, shape


def plain(shape, kind):
    return shape, kind, None


def fronts_call(lengths, tokens, block_grads, weights):
    held, lazies, outs, scratch = [], [], [], []
    for t, token, grad, w in zip((IMAGE, TEXT), tokens, block_grads, weights):
        rows, width, hidden = t.rows, t.width, t.hidden
        held += [token, w[0], w[1], w[4], w[5], w[8], w[9], grad]
        lazies += [all_of(w[i]) for i in (2, 3, 6, 7, 10)]
        outs += [
            staged((2 * width, t.lanes), BF16),
            staged((BATCH, t.padded, 3 * width), BF16),
            staged((BATCH, t.heads // 2, t.padded, 2 * t.padded), BF16),
            staged((rows, width), F32),
            plain((BATCH, EMBED), BF16),
        ]
        scratch += [
            ((3 * width // 128, t.spread, 128), F32),
            ((width // 128, t.spread, 128), F32),
            ((rows, width), BF16),
            ((rows, width), BF16),
        ]
    lazies = [lazies[i] for i in (5, 6, 0, 7, 8, 9, 1, 2, 3, 4)]
    outs.append(plain((BATCH, ROW_TOTAL), F32))
    outs.append(plain((DEVS, BATCH, 2 * EMBED), BF16))
    results = lazy_call(fronts_kernel, "fronts", (lengths,), held, lazies, outs, scratch, ahead=6)
    return results[:5], results[5:10], results[10], results[11]


def middle(t, name, place, lengths, mixed, block_grad, gain, shift, widen, narrow, after):
    rows, width, hidden = t.rows, t.width, t.hidden
    steps = hidden // t.step
    outs = (
        ((width, t.lanes), BF16),
        ((hidden, t.lanes), BF16),
        ((rows, hidden // 2), BF16),
        ((rows, hidden // 2), BF16),
        ((rows, width // 2), BF16),
        ((rows, width // 2), BF16),
        ((rows, width), F32),
        ((1, width), F32),
        ((1, width), F32),
    )

    def held(shape):
        return pl.BlockSpec(shape, lambda i, *_: (0,) * len(shape))

    def tile(i, place):
        return lax.rem(i + place[0] * (steps // 2), steps)

    out_specs = [held(shape) for shape, _ in outs]
    out_specs[1] = pl.BlockSpec((t.step, t.lanes), lambda i, place, lengths: (tile(i, place), 0))
    out_specs[2] = pl.BlockSpec((rows, t.step), lambda i, *_: (0, jnp.minimum(i, steps // 2 - 1)))
    out_specs[3] = pl.BlockSpec((rows, t.step), lambda i, *_: (0, jnp.maximum(i - steps // 2, 0)))
    in_specs = [held(a.shape) for a in (mixed, block_grad, gain, shift)]
    in_specs.append(pl.BlockSpec((width, t.step), lambda i, place, lengths: (0, tile(i, place))))
    in_specs.append(pl.BlockSpec((t.step, width), lambda i, place, lengths: (tile(i, place), 0)))
    in_specs += [pl.BlockSpec(memory_space=pl.ANY)] * len(after)

    def kernel(*refs):
        middle_kernel(t, *refs[:8], *refs[8 + len(after) :])

    return pl.pallas_call(
        kernel,
        name=name + "_middle",
        out_shape=tuple(jax.ShapeDtypeStruct(shape, kind) for shape, kind in outs),
        grid_spec=pltpu.PrefetchScalarGridSpec(
            num_scalar_prefetch=2,
            grid=(steps,),
            in_specs=in_specs,
            out_specs=tuple(out_specs),
            scratch_shapes=[
                pltpu.VMEM((rows, width), BF16),
                pltpu.VMEM((rows, width), BF16),
                pltpu.VMEM((rows, width), F32),
            ],
        ),
        compiler_params=pltpu.CompilerParams(vmem_limit_bytes=VMEM_LIMIT),
        cost_estimate=pl.CostEstimate(flops=1 << 35, bytes_accessed=20 << 20, transcendentals=0),
    )(place, lengths, mixed, block_grad, gain, shift, widen, narrow, *after)


def head_outs(t):
    return [plain((1, t.width), F32)] * 4 + [
        plain((2 * BATCH, t.width + EMBED), F32),
        plain((BATCH, t.width), F32),
        plain((2 * BATCH, t.width), F32),
        plain((2 * BATCH, t.hidden), F32),
    ]


def backs_call(place, lengths, head_in, head_weights, image_row, towers, after):
    held, lazies, outs, scratch = [*head_in], [], head_outs(TEXT), []
    for t, (tokens, gain, arrays) in zip((IMAGE, TEXT), towers):
        rows, width = t.rows, t.width
        held += [tokens, gain]
        if t is IMAGE:
            held.append(image_row)
        lazies += [all_of(a) for a in arrays]
        outs += [
            ((rows, 2 * width), BF16, ()),
            ((rows, 2 * width), BF16, ()),
            staged((t.real, width), F32),
            plain((1, width), F32),
            plain((1, width), F32),
        ]
        scratch += [
            ((width // 128, t.spread, 128), F32),
            ((3 * width // 128, t.spread, 128), F32),
            ((rows, width), F32),
            ((rows, 4 * width), BF16),
        ]
    lazies = [lazies[i] for i in (5, 6, 0, 1, 7, 8, 2, 3, 9, 4)]
    lazies = [all_of(w) for w in head_weights] + lazies
    results = lazy_call(
        backs_kernel, "backs", (place, lengths), held, lazies, outs, scratch, after=after, ahead=8
    )
    return results[:8], results[8:13], results[13:]


def feed(t, place, head, middle, other, buffer, after):
    rows, width = t.rows, t.width
    name = "image" if t is IMAGE else "text"
    own = (middle[0], middle[1], middle[2], middle[4])
    lazies = [all_of(own[0]), all_of(other[0]), all_of(own[2]), all_of(other[2])]
    lazies += [all_of(own[3]), all_of(other[3])]
    for j in range(4):
        some = slice(width * j, width * j + width)
        for side in (own, other):
            lazies.append((side[1], lambda *_, some=some: (some, slice(None)), (width, t.lanes)))
    cols = 256 if t is IMAGE else 512
    scratch = [
        ((width, cols), F32),
        ((width, cols) if t is IMAGE else (8, 128), F32),
        ((width, width // 2), F32),
    ]
    units = IMAGE_FEED_UNITS if t is IMAGE else 8
    total = LATE_UNITS if buffer else units
    (out,) = lazy_call(
        functools.partial(feed_kernel, t, TEXT_FEED_AT if buffer else 0),
        name + "_feed",
        (place,),
        (head[7], head[6]),
        lazies,
        [((DEVS, total, 16, 128), BF16, (DEVS, units, 16, 128))],
        scratch,
        after=after,
        ahead=10,
    )
    return out


def rest(place, factors, vectors, sides, buffer):
    lazies = []
    for own, other in (sides[1], sides[0]):
        lazies += [all_of(a) for a in (*own, *other)]
    outs = [((DEVS, LATE_UNITS, 16, 128), BF16, ())]
    scratch = [
        ((768, 256), F32),
        ((768, 256), F32),
        ((512, 512), F32),
        ((768, 128), F32),
        ((768, 128), F32),
        ((512, 256), F32),
        ((DEVS, 16, 128), F32),
        ((DEVS, 3, 16, 128), BF16),
        ((DEVS, 4, 16, 128), BF16),
        ((DEVS, 9, 16, 128), BF16),
    ]
    (out,) = lazy_call(
        rest_kernel, "rest", (place,), [*factors, *vectors], lazies, outs, scratch, buffer=buffer, ahead=4
    )
    return out


def sum_blocks(pieces):
    lazies, steps = [], []
    for received, step in pieces:
        devices, units = received.shape[:2]
        for at in range(0, units, step):
            some = slice(at, at + step)
            lazies.append(
                (received, lambda *_, some=some: (slice(None), some), (devices, step, 16, 128))
            )
            steps.append(step)

    def body(scalars, held, blocks, outs, scratch):
        at = 0
        for step, block in zip(steps, blocks):
            total = jnp.sum(block.get()[...].astype(F32), axis=0)
            outs[0][at : at + 16 * step, :] = total.reshape(16 * step, 128)
            at += 16 * step

    outs = [plain((16 * sum(steps), 128), F32)]
    return lazy_call(body, "sum_blocks", (), (), lazies, outs, flops=1 << 34, ahead=len(lazies))[0]


def behind(arrays, after):
    def kernel(*refs):
        pass

    any_spec = pl.BlockSpec(memory_space=pl.ANY)
    return pl.pallas_call(
        kernel,
        name="behind",
        out_shape=[jax.ShapeDtypeStruct(array.shape, array.dtype) for array in arrays],
        in_specs=[any_spec] * (len(arrays) + len(after)),
        out_specs=[any_spec] * len(arrays),
        input_output_aliases={i: i for i in range(len(arrays))},
    )(*arrays, *after)


SWAP = [(0, 1), (1, 0)]


def by_token(tokens):
    return tokens.transpose(1, 0, 2).reshape(-1, tokens.shape[2])


def shards(*args):
    image_tokens, image_weights, image_block_grad = args[0], args[1:12], args[12]
    text_tokens, caption_lengths = args[13], args[14]
    text_weights, text_block_grad, log_scale = args[15:26], args[26], args[27]
    core = lax.axis_index("tower")
    dp = lax.axis_index("dp")
    place = jnp.stack([core, dp]).astype(jnp.int32)
    tokens = (by_token(image_tokens), by_token(text_tokens))
    block_grads = (by_token(image_block_grad), by_token(text_block_grad))
    weights = (image_weights, text_weights)
    kinds = ((0, IMAGE, "image"), (1, TEXT, "text"))
    *fronts, kept, copies = fronts_call(caption_lengths, tokens, block_grads, weights)
    units = [f[4] for f in fronts]
    own = lax.all_to_all(copies, "dp", 0, 0, tiled=True).reshape(DEVS * BATCH, 2 * EMBED)

    def swap(*arrays):
        return [lax.ppermute(array, "tower", SWAP) for array in arrays]

    def middle_of(i, after):
        _, t, name = kinds[i]
        w = weights[i]
        return middle(
            t, name, place, caption_lengths, fronts[i][3], block_grads[i], w[4], w[5], w[6], w[7], after
        )

    (kept_other,) = swap(kept)
    image_middle = list(middle_of(0, ()))
    (own,) = behind([own], (image_middle[0], kept_other))
    (other,) = swap(own)
    sent = (0, 1, 3, 5)
    for k, array in zip(sent, behind([image_middle[k] for k in sent], (other,))):
        image_middle[k] = array
    image_sent = swap(*[image_middle[k] for k in sent])

    w = image_weights
    paired = lazy_call(
        pair_kernel,
        "pairs",
        (place, log_scale),
        [own, other, kept, kept_other, w[8], w[9], w[4], w[5]],
        [all_of(w[10]), all_of(w[7]), all_of(w[6])],
        [plain((1, 128), F32), plain((1, 128), F32), plain((2 * BATCH, EMBED), F32), *head_outs(IMAGE)],
        ahead=6,
    )
    loss, scale_grad = paired[0][0, :1], paired[1][0, :1]
    image_head = paired[3:]
    image_feed = feed(IMAGE, place, image_head, image_middle, image_sent, False, ())
    feed_total = lax.all_to_all(image_feed, "dp", 0, 0, tiled=True)
    text_middle = middle_of(1, (image_feed,))
    middles = (image_middle, text_middle)

    back_in = []
    for i, _, _ in kinds:
        f, m, w = fronts[i], middles[i], weights[i]
        back_in.append((tokens[i], w[0], (w[3], m[6], f[1], f[2], w[2])))
    w = text_weights
    text_head, *backs = backs_call(
        place,
        caption_lengths,
        [paired[2], kept, kept_other, w[8], w[9], w[4], w[5]],
        [w[10], w[7], w[6]],
        image_head[5],
        back_in,
        (text_middle[0],),
    )
    heads = (image_head, text_head)
    text_sent = swap(*[text_middle[k] for k in sent])
    late = feed(TEXT, place, heads[1], text_middle, text_sent, True, (backs[1][0],))
    sides = []
    for f, k in zip(fronts, backs):
        sides.append(((f[0], k[0]), swap(f[0], k[1])))
    vectors = []
    for m, h, k in zip(middles, heads, backs):
        vectors += [k[3], k[4], m[7], h[2], m[8], h[3], h[0], h[1]]
    factors = [heads[0][4], heads[1][4]]
    (late,) = behind([rest(place, factors, vectors, sides, late)], (feed_total,))
    late_total = lax.all_to_all(late, "dp", 0, 0, tiled=True)
    mine = sum_blocks(((feed_total, 6), (late_total, 4)))
    (theirs,) = swap(mine)
    weight_outs = (
        ((12, 2304), F32),
        ((12, 768), F32),
        ((12, 3072), F32),
        ((48, 768), F32),
        ((12, 512), F32),
        ((8, 1536), F32),
        ((8, 512), F32),
        ((8, 2048), F32),
        ((32, 512), F32),
        ((8, 512), F32),
    )
    vector_outs = (((1, 12), F32),) * 6 + (((1, 8), F32),) * 6
    grads = call(unpack_kernel, "unpack", (place,), (mine, theirs), weight_outs + vector_outs)

    def ordered(vectors, weights):
        joint, output, widen, narrow, projection = weights
        v = [x.reshape(-1) for x in vectors]
        return [v[0], v[1], joint, output, v[2], v[3], widen, narrow, v[4], v[5], projection]

    def by_sequence(t, grad):
        return grad.reshape(t.length, BATCH, t.width).transpose(1, 0, 2)

    return (
        loss,
        units[0],
        units[1],
        by_sequence(IMAGE, backs[0][2]),
        *ordered(grads[10:16], grads[:5]),
        by_sequence(TEXT, backs[1][2]),
        *ordered(grads[16:22], grads[5:10]),
        scale_grad,
    )


def solution(mesh):
    spread = P(("tower", "dp"), None, None)
    weights = [P()] * 11
    placed = (spread, *weights, spread, spread, P(("tower", "dp")), *weights, spread, P())
    vector, matrix = P("dp"), P("dp", None)
    grads = [vector, vector, matrix, matrix, vector, vector, matrix, matrix, vector, vector, matrix]
    units = P(("tower", "dp"), None)
    return jax.shard_map(
        shards,
        mesh=mesh,
        in_specs=placed,
        out_specs=(P(), units, units, spread, *grads, spread, *grads, P()),
        check_vma=False,
    )
```

profile of v0, /device:TPU:1, one launch (start us, length us, event | category | flops | bytes accessed | tf_op | source)
XLA Modules:
  0.0 250.0 jit_solution(8505199146062580899)
XLA Ops:
  0.7 18.2 %fronts.1 = (bf16[1536,512]{1,0:T(8,128)(2,1)}, bf16[8,64,2304]{2,1,0:T(8,128)(2,1)}, bf16[8,6,64,128]{3,2,1,0:T(8,128)(2,1)}, f32[416,768]{1,0:T(8,128)}, bf16[...) custom-call(s32[8]{0:T(128)} %refs_1_.6, ...), custom_call_target="tpu_custom_call" | custom-call | flops 8589934592 | bytes 20971520 | tf_op jit(solution)/shard_map/fronts/pallas_call | solution.py:1032
  18.8 1.5 collective-permute-start
  20.3 17.0 %all-to-all-start = ((bf16[64,8,1024]{2,1,0:T(8,128)(2,1)}), bf16[64,8,1024]{2,1,0:T(8,128)(2,1)}, u32[]{:S(2)}, u32[]{:S(2)}) async-start(bf16[64,8,1024]{2,1,0:T(8,128)(2,1)} %get-tuple-element.112), calls=%async_computation | async-start | bytes 2097152 | tf_op jit(solution)/shard_map/all_to_all | solution.py:1286
  37.3 0.6 pad_add_fusion.refs_0_.place
  37.9 14.5 %image_middle.1 = (bf16[768,512]{1,0:T(8,128)(2,1)}, bf16[3072,512]{1,0:T(8,128)(2,1)}, bf16[416,1536]{1,0:T(8,128)(2,1)}, bf16[416,1536]{1,0:T(8,128)(2,1)}, bf...) custom-call(s32[2]{0:T(128)} %pad_add_fusion.refs_0_.place, ...), custom_call_target="tpu_custom_call" | custom-call | flops 34359738368 | bytes 20971520 | tf_op jit(solution)/shard_map/image_middle/pallas_call | solution.py:1116
  52.4 0.0 collective-permute-done.refs_2_.refs_5_.refs_4_
  52.5 4.2 %all-to-all-done = bf16[64,8,1024]{2,1,0:T(8,128)(2,1)} async-done(((bf16[64,8,1024]{2,1,0:T(8,128)(2,1)}), bf16[64,8,1024]{2,1,0:T(8,128)(2,1)}, u32[]{:S(2)}, u32[]{:S(2)}) %all-to-all-start) | async-done | bytes 1048608 | tf_op jit(solution)/shard_map/all_to_all | solution.py:1286
  56.6 1.1 collective-permute-start.1
  57.7 2.5 collective-permute-done.1.refs_3_.refs_4_
  60.2 0.0 copy-start
  60.2 1.0 copy-done
  61.2 0.4 collective-permute-start.5
  61.6 0.1 collective-permute-start.3
  62.4 0.5 collective-permute-start.2
  62.8 0.1 collective-permute-start.4
  63.0 10.8 %pairs.1 = (f32[1,128]{1,0:T(1,128)}, f32[1,128]{1,0:T(1,128)}, f32[16,512]{1,0:T(8,128)}, f32[1,768]{1,0:T(1,128)}, f32[1,768]{1,0:T(1,128)}, /*index=5*/f32[1,...) custom-call(s32[2]{0:T(128)} %pad_add_fusion.refs_0_.place, ...), custom_call_target="tpu_custom_call" | custom-call | flops 8589934592 | bytes 20971520 | tf_op jit(solution)/shard_map/pairs/pallas_call | solution.py:1032
  73.8 0.0 collective-permute-done.4.refs_8_
  73.8 0.0 collective-permute-done.2.refs_4_
  73.8 0.0 collective-permute-done.3.refs_6_
  73.9 0.0 collective-permute-done.5.refs_10_.refs_12_.refs_14_.refs_16_
  73.9 11.4 %image_feed.1.refs_8_ = bf16[64,18,16,128]{3,2,1,0:T(8,128)(2,1)} custom-call(s32[2]{0:T(128)} %pad_add_fusion.refs_0_.place, f32[16,3072]{1,0:T(8,128)} %get-tuple-element.122.refs_1_, f32[16,768]{1,0:T(8,128)} %get-tuple-element.123.refs_2_, bf16[768,512]{1,0:T(8,128)(2,1)} %get-tuple-element.127.refs_3_, bf16[768,512]{1,0:T(8,128)(2,1)} %collective-permute-done.2.refs_4_, ...), custom_call_target="tpu_custom_call" | custom-call | flops 8589934592 | bytes 20971520 | tf_op jit(solution)/shard_map/image_feed/pallas_call | solution.py:1032
  85.3 6.6 %all-to-all-start.1 = ((bf16[64,18,16,128]{3,2,1,0:T(8,128)(2,1)}), bf16[64,18,16,128]{3,2,1,0:T(8,128)(2,1)}, u32[]{:S(2)}, u32[]{:S(2)}) async-start(bf16[64,18,16,128]{3,2,1,0:T(8,128)(2,1)} %image_feed.1.refs_8_), calls=%async_computation.1 | async-start | bytes 9437184 | tf_op jit(solution)/shard_map/all_to_all | solution.py:1320
  92.0 12.6 %text_middle.1 = (bf16[512,640]{1,0:T(8,128)(2,1)}, bf16[2048,640]{1,0:T(8,128)(2,1)}, bf16[640,1024]{1,0:T(8,128)(2,1)}, bf16[640,1024]{1,0:T(8,128)(2,1)}, bf1...) custom-call(s32[2]{0:T(128)} %pad_add_fusion.refs_0_.place, ...), custom_call_target="tpu_custom_call" | custom-call | flops 34359738368 | bytes 20971520 | tf_op jit(solution)/shard_map/text_middle/pallas_call | solution.py:1116
  104.6 0.5 collective-permute-start.13
  105.1 0.1 collective-permute-start.11
  105.1 0.4 collective-permute-start.8
  105.6 0.1 collective-permute-start.10
  105.7 0.4 collective-permute-start.12
  106.1 22.4 %backs.1 = (f32[1,512]{1,0:T(1,128)}, f32[1,512]{1,0:T(1,128)}, f32[1,512]{1,0:T(1,128)}, f32[1,512]{1,0:T(1,128)}, f32[16,1024]{1,0:T(8,128)}, /*index=5*/f32[8...) custom-call(s32[2]{0:T(128)} %pad_add_fusion.refs_0_.place, ...), custom_call_target="tpu_custom_call" | custom-call | flops 8589934592 | bytes 20971520 | tf_op jit(solution)/shard_map/backs/pallas_call | solution.py:1032
  128.5 0.0 collective-permute-done.12.refs_8_
  128.5 0.2 collective-permute-start.6
  128.7 0.0 collective-permute-done.10.refs_4_
  128.7 0.6 collective-permute-start.7
  129.3 0.0 collective-permute-done.11.refs_6_
  129.3 0.1 collective-permute-start.9
  129.4 0.0 collective-permute-done.13.refs_10_.refs_12_.refs_14_.refs_16_
  129.4 10.0 %text_feed.1.refs_27_ = bf16[64,24,16,128]{3,2,1,0:T(8,128)(2,1)} custom-call(s32[2]{0:T(128)} %pad_add_fusion.refs_0_.place, f32[16,2048]{1,0:T(8,128)} %get-tuple-element.165.refs_1_, f32[16,512]{1,0:T(8,128)} %get-tuple-element.166.refs_2_, bf16[512,640]{1,0:T(8,128)(2,1)} %get-tuple-element.139.refs_27_.refs_3_, ...), custom_call_target="tpu_custom_call" | custom-call | flops 8589934592 | bytes 20971520 | tf_op jit(solution)/shard_map/text_feed/pallas_call | solution.py:1032
  139.4 0.0 collective-permute-done.6.refs_21_
  139.4 0.0 collective-permute-done.8.refs_25_
  139.4 0.0 collective-permute-done.9.refs_26_
  139.5 0.0 collective-permute-done.7.refs_22_
  139.5 10.5 %rest.1.refs_0_ = bf16[64,24,16,128]{3,2,1,0:T(8,128)(2,1)} custom-call(s32[2]{0:T(128)} %pad_add_fusion.refs_0_.place, f32[16,1280]{1,0:T(8,128)} %get-tuple-element.141.refs_1_, f32[16,1024]{1,0:T(8,128)} %get-tuple-element.142.refs_2_, f32[1,768]{1,0:T(1,128)} %get-tuple-element.143.refs_3_, ...), custom_call_target="tpu_custom_call", output_to_operand_aliasing={{}: (27, {})} | custom-call | flops 8589934592 | bytes 20971520 | tf_op jit(solution)/shard_map/rest/pallas_call | solution.py:1032
  149.9 5.8 %all-to-all-done.1.refs_1_.refs_0_.refs_2_ = bf16[64,18,16,128]{3,2,1,0:T(8,128)(2,1)} async-done(((bf16[64,18,16,128]{3,2,1,0:T(8,128)(2,1)}), bf16[64,18,16,128]{3,2,1,0:T(8,128)(2,1)}, u32[]{:S(2)}, u32[]{:S(2)}) %all-to-all-start.1) | async-done | bytes 4718624 | tf_op jit(solution)/shard_map/all_to_all | solution.py:1320
  155.7 81.9 %all_to_all.15.refs_3_.refs_4_.refs_5_.refs_6_.refs_7_.refs_8_ = bf16[64,24,16,128]{3,2,1,0:T(8,128)(2,1)} all-to-all(bf16[64,24,16,128]{3,2,1,0:T(8,128)(2,1)} %behind.5), channel_id=1, replica_groups=mesh['tower'=2,'dp'=64] {'dp'}, dimensions={0} | all-to-all | bytes 12582912 | tf_op jit(solution)/shard_map/all_to_all | solution.py:1349
  237.7 5.4 %sum_blocks.1.mine = f32[672,128]{1,0:T(8,128)} custom-call(bf16[64,18,16,128]{3,2,1,0:T(8,128)(2,1)} %all-to-all-done.1.refs_1_.refs_0_.refs_2_, bf16[64,18,16,128]{3,2,1,0:T(8,128)(2,1)} %all-to-all-done.1.refs_1_.refs_0_.refs_2_, bf16[64,18,16,128]{3,2,1,0:T(8,128)(2,1)} %all-to-all-done.1.refs_1_.refs_0_.refs_2_, ...), custom_call_target="tpu_custom_call" | custom-call | flops 17179869184 | bytes 20971520 | tf_op jit(solution)/shard_map/sum_blocks/pallas_call | solution.py:1032
  243.0 2.8 %collective-permute-start.14 = (f32[672,128]{1,0:T(8,128)}, f32[672,128]{1,0:T(8,128)}, u32[]{:S(2)}, u32[]{:S(2)}) collective-permute-start(f32[672,128]{1,0:T(8,128)} %sum_blocks.1.mine), channel_id=1, source_target_pairs={{0,64},{64,0},{1,65},{65,1},{2,66},{66,2},{3,67},{67,3},{4,68},{68... | collective-permute-start | bytes 1032200 | tf_op jit(solution)/shard_map/ppermute | solution.py:1289
  245.8 1.6 collective-permute-done.14.other
  247.5 2.3 unpack.1
  (3 shorter events, 0.0 us)
Async XLA Ops:
  18.8 33.6 %collective-permute-start = (f32[8,11008]{1,0:T(8,128)}, f32[8,11008]{1,0:T(8,128)}, u32[]{:S(2)}, u32[]{:S(2)}) collective-permute-start(f32[8,11008]{1,0:T(8,128)} %get-tuple-element.115.refs_4_.refs_3_), channel_id=1, source_target_pairs={{0,64},{64,0},{1,65},{65,1},{2,66},{66,2},{3,67},{67,3},{4,68},{68... | collective-permute-start | bytes 1056776 | tf_op jit(solution)/shard_map/ppermute | solution.py:1289
  20.3 36.3 %all-to-all-start = ((bf16[64,8,1024]{2,1,0:T(8,128)(2,1)}), bf16[64,8,1024]{2,1,0:T(8,128)(2,1)}, u32[]{:S(2)}, u32[]{:S(2)}) async-start(bf16[64,8,1024]{2,1,0:T(8,128)(2,1)} %get-tuple-element.112), calls=%async_computation | async-start | bytes 2097152 | tf_op jit(solution)/shard_map/all_to_all | solution.py:1286
  56.6 3.6 %collective-permute-start.1 = (bf16[512,1024]{1,0:T(8,128)(2,1)}, bf16[512,1024]{1,0:T(8,128)(2,1)S(1)}, u32[]{:S(2)}, u32[]{:S(2)}) collective-permute-start(bf16[512,1024]{1,0:T(8,128)(2,1)} %behind.3.refs_2_), channel_id=1, source_target_pairs={{0,64},{64,0},{1,65},{65,1},{2,66},{66,2},{3,67},{67,3},{4,68},{68... | collective-permute-start | bytes 3145736 | tf_op jit(solution)/shard_map/ppermute | solution.py:1289
  60.2 1.0 copy-start
  61.2 12.6 %collective-permute-start.5 = (bf16[3072,512]{1,0:T(8,128)(2,1)}, bf16[3072,512]{1,0:T(8,128)(2,1)}, u32[]{:S(2)}, u32[]{:S(2)}) collective-permute-start(bf16[3072,512]{1,0:T(8,128)(2,1)} %get-tuple-element.132.refs_9_.refs_11_.refs_13_.refs_15_), channel_id=1, source_target_pairs={{0,64},{64,0},{1,65},{65,1},{2,66},{66,2},{3,67},{67,3},{4,68},{68... | collective-permute-start | bytes 9437192 | tf_op jit(solution)/shard_map/ppermute | solution.py:1289
  61.6 12.3 %collective-permute-start.3 = (bf16[416,1536]{1,0:T(8,128)(2,1)}, bf16[416,1536]{1,0:T(8,128)(2,1)}, u32[]{:S(2)}, u32[]{:S(2)}) collective-permute-start(bf16[416,1536]{1,0:T(8,128)(2,1)} %get-tuple-element.129), channel_id=1, source_target_pairs={{0,64},{64,0},{1,65},{65,1},{2,66},{66,2},{3,67},{67,3},{4,68},{68... | collective-permute-start | bytes 3833864 | tf_op jit(solution)/shard_map/ppermute | solution.py:1289
  62.4 11.5 %collective-permute-start.2 = (bf16[768,512]{1,0:T(8,128)(2,1)}, bf16[768,512]{1,0:T(8,128)(2,1)}, u32[]{:S(2)}, u32[]{:S(2)}) collective-permute-start(bf16[768,512]{1,0:T(8,128)(2,1)} %get-tuple-element.127.refs_3_), channel_id=1, source_target_pairs={{0,64},{64,0},{1,65},{65,1},{2,66},{66,2},{3,67},{67,3},{4,68},{68... | collective-permute-start | bytes 2359304 | tf_op jit(solution)/shard_map/ppermute | solution.py:1289
  62.8 11.0 %collective-permute-start.4 = (bf16[416,384]{1,0:T(8,128)(2,1)}, bf16[416,384]{1,0:T(8,128)(2,1)}, u32[]{:S(2)}, u32[]{:S(2)}) collective-permute-start(bf16[416,384]{1,0:T(8,128)(2,1)} %get-tuple-element.131), channel_id=1, source_target_pairs={{0,64},{64,0},{1,65},{65,1},{2,66},{66,2},{3,67},{67,3},{4,68},{68... | collective-permute-start | bytes 958472 | tf_op jit(solution)/shard_map/ppermute | solution.py:1289
  85.3 70.4 %all-to-all-start.1 = ((bf16[64,18,16,128]{3,2,1,0:T(8,128)(2,1)}), bf16[64,18,16,128]{3,2,1,0:T(8,128)(2,1)}, u32[]{:S(2)}, u32[]{:S(2)}) async-start(bf16[64,18,16,128]{3,2,1,0:T(8,128)(2,1)} %image_feed.1.refs_8_), calls=%async_computation.1 | async-start | bytes 9437184 | tf_op jit(solution)/shard_map/all_to_all | solution.py:1320
  104.6 24.8 %collective-permute-start.13 = (bf16[2048,640]{1,0:T(8,128)(2,1)}, bf16[2048,640]{1,0:T(8,128)(2,1)}, u32[]{:S(2)}, u32[]{:S(2)}) collective-permute-start(bf16[2048,640]{1,0:T(8,128)(2,1)} %get-tuple-element.171.refs_9_.refs_11_.refs_13_.refs_15_), channel_id=1, source_target_pairs={{0,64},{64,0},{1,65},{65,1},{2,66},{66,2},{3,67},{67,3},{4,68},{68... | collective-permute-start | bytes 7864328 | tf_op jit(solution)/shard_map/ppermute | solution.py:1289
  105.1 24.2 %collective-permute-start.11 = (bf16[640,1024]{1,0:T(8,128)(2,1)}, bf16[640,1024]{1,0:T(8,128)(2,1)}, u32[]{:S(2)}, u32[]{:S(2)}) collective-permute-start(bf16[640,1024]{1,0:T(8,128)(2,1)} %get-tuple-element.168), channel_id=1, source_target_pairs={{0,64},{64,0},{1,65},{65,1},{2,66},{66,2},{3,67},{67,3},{4,68},{68... | collective-permute-start | bytes 3932168 | tf_op jit(solution)/shard_map/ppermute | solution.py:1289
  105.1 34.3 %collective-permute-start.8 = (bf16[1536,512]{1,0:T(8,128)(2,1)}, bf16[1536,512]{1,0:T(8,128)(2,1)}, u32[]{:S(2)}, u32[]{:S(2)}) collective-permute-start(bf16[1536,512]{1,0:T(8,128)(2,1)} %get-tuple-element.162.refs_23_), channel_id=1, source_target_pairs={{0,64},{64,0},{1,65},{65,1},{2,66},{66,2},{3,67},{67,3},{4,68},{68... | collective-permute-start | bytes 4718600 | tf_op jit(solution)/shard_map/ppermute | solution.py:1289
  105.6 23.1 %collective-permute-start.10 = (bf16[512,640]{1,0:T(8,128)(2,1)}, bf16[512,640]{1,0:T(8,128)(2,1)}, u32[]{:S(2)}, u32[]{:S(2)}) collective-permute-start(bf16[512,640]{1,0:T(8,128)(2,1)} %get-tuple-element.139.refs_27_.refs_3_), channel_id=1, source_target_pairs={{0,64},{64,0},{1,65},{65,1},{2,66},{66,2},{3,67},{67,3},{4,68},{68... | collective-permute-start | bytes 1966088 | tf_op jit(solution)/shard_map/ppermute | solution.py:1289
  105.7 22.9 %collective-permute-start.12 = (bf16[640,256]{1,0:T(8,128)(2,1)}, bf16[640,256]{1,0:T(8,128)(2,1)}, u32[]{:S(2)}, u32[]{:S(2)}) collective-permute-start(bf16[640,256]{1,0:T(8,128)(2,1)} %get-tuple-element.170), channel_id=1, source_target_pairs={{0,64},{64,0},{1,65},{65,1},{2,66},{66,2},{3,67},{67,3},{4,68},{68... | collective-permute-start | bytes 983048 | tf_op jit(solution)/shard_map/ppermute | solution.py:1289
  128.5 10.9 %collective-permute-start.6 = (bf16[1024,640]{1,0:T(8,128)(2,1)}, bf16[1024,640]{1,0:T(8,128)(2,1)}, u32[]{:S(2)}, u32[]{:S(2)}) collective-permute-start(bf16[1024,640]{1,0:T(8,128)(2,1)} %get-tuple-element.159.refs_19_), channel_id=1, source_target_pairs={{0,64},{64,0},{1,65},{65,1},{2,66},{66,2},{3,67},{67,3},{4,68},{68... | collective-permute-start | bytes 3932168 | tf_op jit(solution)/shard_map/ppermute | solution.py:1289
  128.7 10.8 %collective-permute-start.7 = (bf16[640,1024]{1,0:T(8,128)(2,1)}, bf16[640,1024]{1,0:T(8,128)(2,1)}, u32[]{:S(2)}, u32[]{:S(2)}) collective-permute-start(bf16[640,1024]{1,0:T(8,128)(2,1)} %get-tuple-element.161), channel_id=1, source_target_pairs={{0,64},{64,0},{1,65},{65,1},{2,66},{66,2},{3,67},{67,3},{4,68},{68... | collective-permute-start | bytes 3932168 | tf_op jit(solution)/shard_map/ppermute | solution.py:1289
  129.3 10.2 %collective-permute-start.9 = (bf16[416,1536]{1,0:T(8,128)(2,1)}, bf16[416,1536]{1,0:T(8,128)(2,1)}, u32[]{:S(2)}, u32[]{:S(2)}) collective-permute-start(bf16[416,1536]{1,0:T(8,128)(2,1)} %get-tuple-element.164), channel_id=1, source_target_pairs={{0,64},{64,0},{1,65},{65,1},{2,66},{66,2},{3,67},{67,3},{4,68},{68... | collective-permute-start | bytes 3833864 | tf_op jit(solution)/shard_map/ppermute | solution.py:1289
  243.0 4.4 %collective-permute-start.14 = (f32[672,128]{1,0:T(8,128)}, f32[672,128]{1,0:T(8,128)}, u32[]{:S(2)}, u32[]{:S(2)}) collective-permute-start(f32[672,128]{1,0:T(8,128)} %sum_blocks.1.mine), channel_id=1, source_target_pairs={{0,64},{64,0},{1,65},{65,1},{2,66},{66,2},{3,67},{67,3},{4,68},{68... | collective-permute-start | bytes 1032200 | tf_op jit(solution)/shard_map/ppermute | solution.py:1289
where the time goes:
time: 255 us; the launch traced here: 250 us
  Pallas kernels  118 us (46%)
  blocking collectives  81.9 us (32%)
  starting transfers between devices  32.5 us (13%)
  waiting for transfers between devices  14.1 us (6%)
    pallas_call x7, Pallas kernels, lazy_call(): pl.pallas_call(kernel, name=name, out_shape=tuple((jax.ShapeDtypeStruct(s...  88.7 us
    all_to_all x1, blocking collectives, shards(): late_total = lax.all_to_all(late, 'dp', 0, 0, tiled=True)  81.9 us
    pallas_call x2, Pallas kernels, middle(): pl.pallas_call(kernel, name=name + '_middle', out_shape=tuple((jax.ShapeD...  27.1 us
    all_to_all x1, starting transfers between devices, shards(): lax.all_to_all(copies, 'dp', 0, 0, tiled=True)  17 us
    ppermute x15, starting transfers between devices, swap(): return [lax.ppermute(array, 'tower', SWAP) for array in arrays]  8.88 us
    all_to_all x1, starting transfers between devices, shards(): feed_total = lax.all_to_all(image_feed, 'dp', 0, 0, tiled=True)  6.63 us
    all_to_all x1, waiting for transfers between devices, shards(): feed_total = lax.all_to_all(image_feed, 'dp', 0, 0, tiled=True)  5.8 us
  transfers between devices with their start and end apart: 17, of which 4 were waited for; matrix products, arithmetic and copies ran while one was open for 0% of the time, Pallas kernels for 32%

commit v1 on v0

--- a/solution.py
+++ b/solution.py
@@ -1252,7 +1252,7 @@
     def kernel(*refs):
         pass
 
-    any_spec = pl.BlockSpec(memory_space=pl.ANY)
+    any_spec = pl.BlockSpec(memory_space=pltpu.HBM)
     return pl.pallas_call(
         kernel,
         name="behind",
@@ -1347,7 +1347,7 @@
     factors = [heads[0][4], heads[1][4]]
     (late,) = behind([rest(place, factors, vectors, sides, late)], (feed_total,))
     late_total = lax.all_to_all(late, "dp", 0, 0, tiled=True)
-    mine = sum_blocks(((feed_total, 6), (late_total, 4)))
+    mine = sum_blocks(((feed_total, 3), (late_total, 3)))
     (theirs,) = swap(mine)
     weight_outs = (
         ((12, 2304), F32),

time: 255 us -> 255 us (level)
  no operation moved by 1% of the time
where the time goes in v1:
time: 255 us; the launch traced here: 250 us
  Pallas kernels  118 us (46%)
  blocking collectives  81.9 us (32%)
  starting transfers between devices  32.5 us (13%)
  waiting for transfers between devices  14.1 us (6%)
    pallas_call x7, Pallas kernels, lazy_call(): pl.pallas_call(kernel, name=name, out_shape=tuple((jax.ShapeDtypeStruct(s...  88.8 us
    all_to_all x1, blocking collectives, shards(): late_total = lax.all_to_all(late, 'dp', 0, 0, tiled=True)  81.9 us
    pallas_call x2, Pallas kernels, middle(): pl.pallas_call(kernel, name=name + '_middle', out_shape=tuple((jax.ShapeD...  27.1 us
    all_to_all x1, starting transfers between devices, shards(): lax.all_to_all(copies, 'dp', 0, 0, tiled=True)  17 us
    ppermute x15, starting transfers between devices, swap(): return [lax.ppermute(array, 'tower', SWAP) for array in arrays]  8.88 us
    all_to_all x1, starting transfers between devices, shards(): feed_total = lax.all_to_all(image_feed, 'dp', 0, 0, tiled=True)  6.63 us
    all_to_all x1, waiting for transfers between devices, shards(): feed_total = lax.all_to_all(image_feed, 'dp', 0, 0, tiled=True)  5.8 us
  transfers between devices with their start and end apart: 17, of which 4 were waited for; matrix products, arithmetic and copies ran while one was open for 0% of the time, Pallas kernels for 32%

profile of v1, /device:TPU:1, one launch (start us, length us, event | category | flops | bytes accessed | tf_op | source)
XLA Modules:
  0.0 250.0 jit_solution(2875643447812321988)
XLA Ops:
  0.7 18.2 %fronts.1 = (bf16[1536,512]{1,0:T(8,128)(2,1)}, bf16[8,64,2304]{2,1,0:T(8,128)(2,1)}, bf16[8,6,64,128]{3,2,1,0:T(8,128)(2,1)}, f32[416,768]{1,0:T(8,128)}, bf16[...) custom-call(s32[8]{0:T(128)} %refs_1_.6, ...), custom_call_target="tpu_custom_call" | custom-call | flops 8589934592 | bytes 20971520 | tf_op jit(solution)/shard_map/fronts/pallas_call | solution.py:1032
  18.8 1.5 collective-permute-start
  20.3 17.0 %all-to-all-start = ((bf16[64,8,1024]{2,1,0:T(8,128)(2,1)}), bf16[64,8,1024]{2,1,0:T(8,128)(2,1)}, u32[]{:S(2)}, u32[]{:S(2)}) async-start(bf16[64,8,1024]{2,1,0:T(8,128)(2,1)} %get-tuple-element.112), calls=%async_computation | async-start | bytes 2097152 | tf_op jit(solution)/shard_map/all_to_all | solution.py:1286
  37.3 0.6 pad_add_fusion.refs_0_.place
  37.9 14.5 %image_middle.1 = (bf16[768,512]{1,0:T(8,128)(2,1)}, bf16[3072,512]{1,0:T(8,128)(2,1)}, bf16[416,1536]{1,0:T(8,128)(2,1)}, bf16[416,1536]{1,0:T(8,128)(2,1)}, bf...) custom-call(s32[2]{0:T(128)} %pad_add_fusion.refs_0_.place, ...), custom_call_target="tpu_custom_call" | custom-call | flops 34359738368 | bytes 20971520 | tf_op jit(solution)/shard_map/image_middle/pallas_call | solution.py:1116
  52.4 0.0 collective-permute-done.refs_2_.refs_5_.refs_4_
  52.5 4.2 %all-to-all-done = bf16[64,8,1024]{2,1,0:T(8,128)(2,1)} async-done(((bf16[64,8,1024]{2,1,0:T(8,128)(2,1)}), bf16[64,8,1024]{2,1,0:T(8,128)(2,1)}, u32[]{:S(2)}, u32[]{:S(2)}) %all-to-all-start) | async-done | bytes 1048608 | tf_op jit(solution)/shard_map/all_to_all | solution.py:1286
  56.6 1.1 collective-permute-start.1
  57.7 2.5 collective-permute-done.1.refs_3_.refs_4_
  60.2 0.0 copy-start
  60.2 1.0 copy-done
  61.2 0.4 collective-permute-start.5
  61.6 0.1 collective-permute-start.3
  62.4 0.5 collective-permute-start.2
  62.8 0.1 collective-permute-start.4
  63.0 10.8 %pairs.1 = (f32[1,128]{1,0:T(1,128)}, f32[1,128]{1,0:T(1,128)}, f32[16,512]{1,0:T(8,128)}, f32[1,768]{1,0:T(1,128)}, f32[1,768]{1,0:T(1,128)}, /*index=5*/f32[1,...) custom-call(s32[2]{0:T(128)} %pad_add_fusion.refs_0_.place, ...), custom_call_target="tpu_custom_call" | custom-call | flops 8589934592 | bytes 20971520 | tf_op jit(solution)/shard_map/pairs/pallas_call | solution.py:1032
  73.8 0.0 collective-permute-done.4.refs_8_
  73.8 0.0 collective-permute-done.2.refs_4_
  73.8 0.0 collective-permute-done.3.refs_6_
  73.9 0.0 collective-permute-done.5.refs_10_.refs_12_.refs_14_.refs_16_
  73.9 11.4 %image_feed.1.refs_8_ = bf16[64,18,16,128]{3,2,1,0:T(8,128)(2,1)} custom-call(s32[2]{0:T(128)} %pad_add_fusion.refs_0_.place, f32[16,3072]{1,0:T(8,128)} %get-tuple-element.122.refs_1_, f32[16,768]{1,0:T(8,128)} %get-tuple-element.123.refs_2_, bf16[768,512]{1,0:T(8,128)(2,1)} %get-tuple-element.127.refs_3_, bf16[768,512]{1,0:T(8,128)(2,1)} %collective-permute-done.2.refs_4_, ...), custom_call_target="tpu_custom_call" | custom-call | flops 8589934592 | bytes 20971520 | tf_op jit(solution)/shard_map/image_feed/pallas_call | solution.py:1032
  85.3 6.6 %all-to-all-start.1 = ((bf16[64,18,16,128]{3,2,1,0:T(8,128)(2,1)}), bf16[64,18,16,128]{3,2,1,0:T(8,128)(2,1)}, u32[]{:S(2)}, u32[]{:S(2)}) async-start(bf16[64,18,16,128]{3,2,1,0:T(8,128)(2,1)} %image_feed.1.refs_8_), calls=%async_computation.1 | async-start | bytes 9437184 | tf_op jit(solution)/shard_map/all_to_all | solution.py:1320
  92.0 12.6 %text_middle.1 = (bf16[512,640]{1,0:T(8,128)(2,1)}, bf16[2048,640]{1,0:T(8,128)(2,1)}, bf16[640,1024]{1,0:T(8,128)(2,1)}, bf16[640,1024]{1,0:T(8,128)(2,1)}, bf1...) custom-call(s32[2]{0:T(128)} %pad_add_fusion.refs_0_.place, ...), custom_call_target="tpu_custom_call" | custom-call | flops 34359738368 | bytes 20971520 | tf_op jit(solution)/shard_map/text_middle/pallas_call | solution.py:1116
  104.6 0.5 collective-permute-start.13
  105.1 0.1 collective-permute-start.11
  105.1 0.4 collective-permute-start.8
  105.6 0.1 collective-permute-start.10
  105.7 0.4 collective-permute-start.12
  106.1 22.4 %backs.1 = (f32[1,512]{1,0:T(1,128)}, f32[1,512]{1,0:T(1,128)}, f32[1,512]{1,0:T(1,128)}, f32[1,512]{1,0:T(1,128)}, f32[16,1024]{1,0:T(8,128)}, /*index=5*/f32[8...) custom-call(s32[2]{0:T(128)} %pad_add_fusion.refs_0_.place, ...), custom_call_target="tpu_custom_call" | custom-call | flops 8589934592 | bytes 20971520 | tf_op jit(solution)/shard_map/backs/pallas_call | solution.py:1032
  128.5 0.0 collective-permute-done.12.refs_8_
  128.5 0.2 collective-permute-start.6
  128.7 0.0 collective-permute-done.10.refs_4_
  128.7 0.6 collective-permute-start.7
  129.3 0.0 collective-permute-done.11.refs_6_
  129.3 0.1 collective-permute-start.9
  129.4 0.0 collective-permute-done.13.refs_10_.refs_12_.refs_14_.refs_16_
  129.4 10.0 %text_feed.1.refs_27_ = bf16[64,24,16,128]{3,2,1,0:T(8,128)(2,1)} custom-call(s32[2]{0:T(128)} %pad_add_fusion.refs_0_.place, f32[16,2048]{1,0:T(8,128)} %get-tuple-element.165.refs_1_, f32[16,512]{1,0:T(8,128)} %get-tuple-element.166.refs_2_, bf16[512,640]{1,0:T(8,128)(2,1)} %get-tuple-element.139.refs_27_.refs_3_, ...), custom_call_target="tpu_custom_call" | custom-call | flops 8589934592 | bytes 20971520 | tf_op jit(solution)/shard_map/text_feed/pallas_call | solution.py:1032
  139.4 0.0 collective-permute-done.6.refs_21_
  139.4 0.0 collective-permute-done.8.refs_25_
  139.4 0.0 collective-permute-done.9.refs_26_
  139.5 0.0 collective-permute-done.7.refs_22_
  139.5 10.5 %rest.1.refs_0_ = bf16[64,24,16,128]{3,2,1,0:T(8,128)(2,1)} custom-call(s32[2]{0:T(128)} %pad_add_fusion.refs_0_.place, f32[16,1280]{1,0:T(8,128)} %get-tuple-element.141.refs_1_, f32[16,1024]{1,0:T(8,128)} %get-tuple-element.142.refs_2_, f32[1,768]{1,0:T(1,128)} %get-tuple-element.143.refs_3_, ...), custom_call_target="tpu_custom_call", output_to_operand_aliasing={{}: (27, {})} | custom-call | flops 8589934592 | bytes 20971520 | tf_op jit(solution)/shard_map/rest/pallas_call | solution.py:1032
  149.9 5.8 %all-to-all-done.1.refs_1_.refs_0_.refs_2_.refs_3_.refs_4_.refs_5_ = bf16[64,18,16,128]{3,2,1,0:T(8,128)(2,1)} async-done(((bf16[64,18,16,128]{3,2,1,0:T(8,128)(2,1)}), bf16[64,18,16,128]{3,2,1,0:T(8,128)(2,1)}, u32[]{:S(2)}, u32[]{:S(2)}) %all-to-all-start.1) | async-done | bytes 4718624 | tf_op jit(solution)/shard_map/all_to_all | solution.py:1320
  155.7 81.9 %all_to_all.15.refs_6_.refs_7_.refs_8_.refs_9_.refs_10_.refs_11_.refs_12_.refs_13_ = bf16[64,24,16,128]{3,2,1,0:T(8,128)(2,1)} all-to-all(bf16[64,24,16,128]{3,2,1,0:T(8,128)(2,1)} %behind.5), channel_id=1, replica_groups=mesh['tower'=2,'dp'=64] {'dp'}, dimensions={0} | all-to-all | bytes 12582912 | tf_op jit(solution)/shard_map/all_to_all | solution.py:1349
  237.7 5.4 %sum_blocks.1.mine = f32[672,128]{1,0:T(8,128)} custom-call(bf16[64,18,16,128]{3,2,1,0:T(8,128)(2,1)} %all-to-all-done.1.refs_1_.refs_0_.refs_2_.refs_3_.refs_4_.refs_5_, bf16[64,18,16,128]{3,2,1,0:T(8,128)(2,1)} %all-to-all-done.1.refs_1_.refs_0_.refs_2_.refs_3_.refs_4_.refs_5_, ...), custom_call_target="tpu_custom_call" | custom-call | flops 17179869184 | bytes 20971520 | tf_op jit(solution)/shard_map/sum_blocks/pallas_call | solution.py:1032
  243.1 2.8 %collective-permute-start.14 = (f32[672,128]{1,0:T(8,128)}, f32[672,128]{1,0:T(8,128)}, u32[]{:S(2)}, u32[]{:S(2)}) collective-permute-start(f32[672,128]{1,0:T(8,128)} %sum_blocks.1.mine), channel_id=1, source_target_pairs={{0,64},{64,0},{1,65},{65,1},{2,66},{66,2},{3,67},{67,3},{4,68},{68... | collective-permute-start | bytes 1032200 | tf_op jit(solution)/shard_map/ppermute | solution.py:1289
  245.9 1.6 collective-permute-done.14.other
  247.5 2.3 unpack.1
  (3 shorter events, 0.0 us)
Async XLA Ops:
  18.8 33.6 %collective-permute-start = (f32[8,11008]{1,0:T(8,128)}, f32[8,11008]{1,0:T(8,128)}, u32[]{:S(2)}, u32[]{:S(2)}) collective-permute-start(f32[8,11008]{1,0:T(8,128)} %get-tuple-element.115.refs_4_.refs_3_), channel_id=1, source_target_pairs={{0,64},{64,0},{1,65},{65,1},{2,66},{66,2},{3,67},{67,3},{4,68},{68... | collective-permute-start | bytes 1056776 | tf_op jit(solution)/shard_map/ppermute | solution.py:1289
  20.3 36.3 %all-to-all-start = ((bf16[64,8,1024]{2,1,0:T(8,128)(2,1)}), bf16[64,8,1024]{2,1,0:T(8,128)(2,1)}, u32[]{:S(2)}, u32[]{:S(2)}) async-start(bf16[64,8,1024]{2,1,0:T(8,128)(2,1)} %get-tuple-element.112), calls=%async_computation | async-start | bytes 2097152 | tf_op jit(solution)/shard_map/all_to_all | solution.py:1286
  56.6 3.6 %collective-permute-start.1 = (bf16[512,1024]{1,0:T(8,128)(2,1)}, bf16[512,1024]{1,0:T(8,128)(2,1)S(1)}, u32[]{:S(2)}, u32[]{:S(2)}) collective-permute-start(bf16[512,1024]{1,0:T(8,128)(2,1)} %behind.3.refs_2_), channel_id=1, source_target_pairs={{0,64},{64,0},{1,65},{65,1},{2,66},{66,2},{3,67},{67,3},{4,68},{68... | collective-permute-start | bytes 3145736 | tf_op jit(solution)/shard_map/ppermute | solution.py:1289
  60.2 1.0 copy-start
  61.2 12.6 %collective-permute-start.5 = (bf16[3072,512]{1,0:T(8,128)(2,1)}, bf16[3072,512]{1,0:T(8,128)(2,1)}, u32[]{:S(2)}, u32[]{:S(2)}) collective-permute-start(bf16[3072,512]{1,0:T(8,128)(2,1)} %get-tuple-element.132.refs_9_.refs_11_.refs_13_.refs_15_), channel_id=1, source_target_pairs={{0,64},{64,0},{1,65},{65,1},{2,66},{66,2},{3,67},{67,3},{4,68},{68... | collective-permute-start | bytes 9437192 | tf_op jit(solution)/shard_map/ppermute | solution.py:1289
  61.6 12.3 %collective-permute-start.3 = (bf16[416,1536]{1,0:T(8,128)(2,1)}, bf16[416,1536]{1,0:T(8,128)(2,1)}, u32[]{:S(2)}, u32[]{:S(2)}) collective-permute-start(bf16[416,1536]{1,0:T(8,128)(2,1)} %get-tuple-element.129), channel_id=1, source_target_pairs={{0,64},{64,0},{1,65},{65,1},{2,66},{66,2},{3,67},{67,3},{4,68},{68... | collective-permute-start | bytes 3833864 | tf_op jit(solution)/shard_map/ppermute | solution.py:1289
  62.4 11.5 %collective-permute-start.2 = (bf16[768,512]{1,0:T(8,128)(2,1)}, bf16[768,512]{1,0:T(8,128)(2,1)}, u32[]{:S(2)}, u32[]{:S(2)}) collective-permute-start(bf16[768,512]{1,0:T(8,128)(2,1)} %get-tuple-element.127.refs_3_), channel_id=1, source_target_pairs={{0,64},{64,0},{1,65},{65,1},{2,66},{66,2},{3,67},{67,3},{4,68},{68... | collective-permute-start | bytes 2359304 | tf_op jit(solution)/shard_map/ppermute | solution.py:1289
  62.8 11.0 %collective-permute-start.4 = (bf16[416,384]{1,0:T(8,128)(2,1)}, bf16[416,384]{1,0:T(8,128)(2,1)}, u32[]{:S(2)}, u32[]{:S(2)}) collective-permute-start(bf16[416,384]{1,0:T(8,128)(2,1)} %get-tuple-element.131), channel_id=1, source_target_pairs={{0,64},{64,0},{1,65},{65,1},{2,66},{66,2},{3,67},{67,3},{4,68},{68... | collective-permute-start | bytes 958472 | tf_op jit(solution)/shard_map/ppermute | solution.py:1289
  85.3 70.4 %all-to-all-start.1 = ((bf16[64,18,16,128]{3,2,1,0:T(8,128)(2,1)}), bf16[64,18,16,128]{3,2,1,0:T(8,128)(2,1)}, u32[]{:S(2)}, u32[]{:S(2)}) async-start(bf16[64,18,16,128]{3,2,1,0:T(8,128)(2,1)} %image_feed.1.refs_8_), calls=%async_computation.1 | async-start | bytes 9437184 | tf_op jit(solution)/shard_map/all_to_all | solution.py:1320
  104.6 24.8 %collective-permute-start.13 = (bf16[2048,640]{1,0:T(8,128)(2,1)}, bf16[2048,640]{1,0:T(8,128)(2,1)}, u32[]{:S(2)}, u32[]{:S(2)}) collective-permute-start(bf16[2048,640]{1,0:T(8,128)(2,1)} %get-tuple-element.171.refs_9_.refs_11_.refs_13_.refs_15_), channel_id=1, source_target_pairs={{0,64},{64,0},{1,65},{65,1},{2,66},{66,2},{3,67},{67,3},{4,68},{68... | collective-permute-start | bytes 7864328 | tf_op jit(solution)/shard_map/ppermute | solution.py:1289
  105.1 24.2 %collective-permute-start.11 = (bf16[640,1024]{1,0:T(8,128)(2,1)}, bf16[640,1024]{1,0:T(8,128)(2,1)}, u32[]{:S(2)}, u32[]{:S(2)}) collective-permute-start(bf16[640,1024]{1,0:T(8,128)(2,1)} %get-tuple-element.168), channel_id=1, source_target_pairs={{0,64},{64,0},{1,65},{65,1},{2,66},{66,2},{3,67},{67,3},{4,68},{68... | collective-permute-start | bytes 3932168 | tf_op jit(solution)/shard_map/ppermute | solution.py:1289
  105.1 34.3 %collective-permute-start.8 = (bf16[1536,512]{1,0:T(8,128)(2,1)}, bf16[1536,512]{1,0:T(8,128)(2,1)}, u32[]{:S(2)}, u32[]{:S(2)}) collective-permute-start(bf16[1536,512]{1,0:T(8,128)(2,1)} %get-tuple-element.162.refs_23_), channel_id=1, source_target_pairs={{0,64},{64,0},{1,65},{65,1},{2,66},{66,2},{3,67},{67,3},{4,68},{68... | collective-permute-start | bytes 4718600 | tf_op jit(solution)/shard_map/ppermute | solution.py:1289
  105.6 23.1 %collective-permute-start.10 = (bf16[512,640]{1,0:T(8,128)(2,1)}, bf16[512,640]{1,0:T(8,128)(2,1)}, u32[]{:S(2)}, u32[]{:S(2)}) collective-permute-start(bf16[512,640]{1,0:T(8,128)(2,1)} %get-tuple-element.139.refs_27_.refs_3_), channel_id=1, source_target_pairs={{0,64},{64,0},{1,65},{65,1},{2,66},{66,2},{3,67},{67,3},{4,68},{68... | collective-permute-start | bytes 1966088 | tf_op jit(solution)/shard_map/ppermute | solution.py:1289
  105.7 22.9 %collective-permute-start.12 = (bf16[640,256]{1,0:T(8,128)(2,1)}, bf16[640,256]{1,0:T(8,128)(2,1)}, u32[]{:S(2)}, u32[]{:S(2)}) collective-permute-start(bf16[640,256]{1,0:T(8,128)(2,1)} %get-tuple-element.170), channel_id=1, source_target_pairs={{0,64},{64,0},{1,65},{65,1},{2,66},{66,2},{3,67},{67,3},{4,68},{68... | collective-permute-start | bytes 983048 | tf_op jit(solution)/shard_map/ppermute | solution.py:1289
  128.5 10.9 %collective-permute-start.6 = (bf16[1024,640]{1,0:T(8,128)(2,1)}, bf16[1024,640]{1,0:T(8,128)(2,1)}, u32[]{:S(2)}, u32[]{:S(2)}) collective-permute-start(bf16[1024,640]{1,0:T(8,128)(2,1)} %get-tuple-element.159.refs_19_), channel_id=1, source_target_pairs={{0,64},{64,0},{1,65},{65,1},{2,66},{66,2},{3,67},{67,3},{4,68},{68... | collective-permute-start | bytes 3932168 | tf_op jit(solution)/shard_map/ppermute | solution.py:1289
  128.7 10.8 %collective-permute-start.7 = (bf16[640,1024]{1,0:T(8,128)(2,1)}, bf16[640,1024]{1,0:T(8,128)(2,1)}, u32[]{:S(2)}, u32[]{:S(2)}) collective-permute-start(bf16[640,1024]{1,0:T(8,128)(2,1)} %get-tuple-element.161), channel_id=1, source_target_pairs={{0,64},{64,0},{1,65},{65,1},{2,66},{66,2},{3,67},{67,3},{4,68},{68... | collective-permute-start | bytes 3932168 | tf_op jit(solution)/shard_map/ppermute | solution.py:1289
  129.3 10.2 %collective-permute-start.9 = (bf16[416,1536]{1,0:T(8,128)(2,1)}, bf16[416,1536]{1,0:T(8,128)(2,1)}, u32[]{:S(2)}, u32[]{:S(2)}) collective-permute-start(bf16[416,1536]{1,0:T(8,128)(2,1)} %get-tuple-element.164), channel_id=1, source_target_pairs={{0,64},{64,0},{1,65},{65,1},{2,66},{66,2},{3,67},{67,3},{4,68},{68... | collective-permute-start | bytes 3833864 | tf_op jit(solution)/shard_map/ppermute | solution.py:1289
  243.1 4.4 %collective-permute-start.14 = (f32[672,128]{1,0:T(8,128)}, f32[672,128]{1,0:T(8,128)}, u32[]{:S(2)}, u32[]{:S(2)}) collective-permute-start(f32[672,128]{1,0:T(8,128)} %sum_blocks.1.mine), channel_id=1, source_target_pairs={{0,64},{64,0},{1,65},{65,1},{2,66},{66,2},{3,67},{67,3},{4,68},{68... | collective-permute-start | bytes 1032200 | tf_op jit(solution)/shard_map/ppermute | solution.py:1289
